TPU v7x, 128 devices: a whole 4x4x4 slice. The times are simulated.
128 devices in a mesh: section: 2 (over z_lo), seq: 8 (over y, z_hi), wa: 8 (over x, core).
Axes of the slice: x: 4, y: 4, z: 4 (z_hi: 2, z_lo: 2; z = z_hi * 2 + z_lo), core: 2. Of those that a mesh axis runs over, the one named last changes fastest.
Arguments:
- first_layer_input: bfloat16 [2, 1536, 1024], P(None, 'wa', 'seq'), may hold values from -6 to 6
- routes: int32 [2, 2, 1024, 8], P('section', None, 'seq'), may hold values from 0 to 39, all different within a row; in each aligned block of 128 rows (0 to 127, 128 to 255, ..., all dimensions but the last counted through in order) at most 32 rows name the same one
- cotangent: bfloat16 [2, 1536, 1024], P(None, 'wa', 'seq'), may hold values from -6 to 6
- gains: float32 [2, 2, 1536], P('section', None, 'wa'), may hold values from 0.1 to 1.9
- qkv_weight: bfloat16 [2, 1536, 2560], P('section', 'wa'), may hold values from -0.15625 to 0.15625
- out_weight: bfloat16 [2, 1536, 1536], P('section', 'wa'), may hold values from -0.875 to 0.875
- router_weight: bfloat16 [2, 1536, 40], P('section', 'wa'), may hold values from -0.078125 to 0.078125
- expert_in: bfloat16 [2, 40, 2, 512, 1536], P('section', None, None, 'wa'), may hold values from -0.15625 to 0.15625
- expert_out: bfloat16 [2, 40, 512, 1536], P('section', None, 'wa'), may hold values from -0.25 to 0.25
Outputs:
- layer_outputs: bfloat16 [2, 2, 1024, 1536], P('section', None, 'seq', 'wa')
- input_grads: float32 [2, 2, 1024, 1536], P('section', None, 'seq', 'wa')
- gain_grads: float32 [2, 2, 1536], P('section', None, 'wa')
- qkv_grads: float32 [2, 1536, 2560], P('section', 'wa', 'seq')
- attn_out_grads: float32 [2, 1536, 1536], P('section', 'wa', 'seq')
- router_grads: float32 [2, 1536, 40], P('section', 'wa')
- expert_in_grads: float32 [2, 40, 2, 512, 1536], P('section', None, None, 'wa', 'seq')
- expert_out_grads: float32 [2, 40, 512, 1536], P('section', None, 'wa', 'seq')
Inputs may be any that keep to these rules, and one draw needn't show every extreme that they name: `routes`: in each aligned block of 128 rows (the rows of one device along seq) no expert is named by more than 32 rows, a bound that some block reaches; the 8 experts of a row differ.
All inputs are finite; a program needn't handle non-finite values.
Results may differ from a plain program's by a relative error of at most 0.04.
Values may be sent and summed in bfloat16 or wider, within the bound.
No kernel may reach another device: no remote copies, remote signals or barrier semaphores. Data moves between devices by JAX's collectives and lax.ppermute only.
A program may use at most 320 MiB of HBM per device.

v0:
```python
import jax
import jax.numpy as jnp
from jax import lax
from jax.sharding import PartitionSpec as P

HEADS = 24
KV_HEADS = 8
HEAD_DIM = 64
EXPERTS = 40
TOP = 8


epsilon = 1e-06


def passed_along(block, axis, distance):
    devices = range(lax.axis_size(axis))
    route = [(i - distance, i) for i in devices if i - distance in devices]
    return lax.ppermute(block, axis, route)


def rotary_angles(positions, head_dim):
    half_dim = head_dim // 2
    frequency = 10000.0 ** (-jnp.arange(half_dim).astype(jnp.float32) * (2.0 / head_dim))
    angles = positions.astype(jnp.float32)[:, None] * frequency[None, :]
    return (jnp.cos(angles), jnp.sin(angles))


def rotate(values, cosine, sine):
    half_dim = values.shape[-1] // 2
    first_half = values[..., :half_dim]
    second_half = values[..., half_dim:]
    cosine = cosine[:, None, :]
    sine = sine[:, None, :]
    return jnp.concatenate(
        [first_half * cosine - second_half * sine, second_half * cosine + first_half * sine],
        axis=-1,
    )


def slot_table(route_ids, capacity):
    count_rows, count_top = route_ids.shape
    flat_ids = route_ids.reshape(-1)
    one_hot = (flat_ids[:, None] == jnp.arange(EXPERTS, dtype=jnp.int32)[None, :]).astype(jnp.int32)
    before = jnp.cumsum(one_hot, axis=0) - one_hot
    places = jnp.sum(before * one_hot, axis=1)
    slots = flat_ids * capacity + places
    sources = jnp.arange(count_rows * count_top, dtype=jnp.int32) // count_top
    owner = jnp.full((EXPERTS * capacity,), count_rows, jnp.int32).at[slots].set(sources)
    return (slots, owner)


def on_device(
    first_layer_input,
    routes,
    cotangent,
    gains,
    qkv_weight,
    out_weight,
    router_weight,
    expert_in,
    expert_out,
):
    section_first = lax.axis_index("section") == 0
    seq_index = lax.axis_index("seq")
    window_attention_index = lax.axis_index("wa")
    seq_count = lax.axis_size("seq")
    wa_count = lax.axis_size("wa")
    microbatch, width_local, rows = first_layer_input.shape
    width = width_local * wa_count
    group_count = KV_HEADS // seq_count
    per_group = HEADS // KV_HEADS
    part_rows = rows // wa_count
    head_rows = part_rows * seq_count
    length = rows * seq_count
    capacity = (rows * TOP * 5 + 4 * EXPERTS - 1) // (4 * EXPERTS)
    attention_score_scale = HEAD_DIM ** (-0.5)
    gain_one = gains[0, 0]
    gain_two = gains[0, 1]
    w_qkv = qkv_weight[0]
    w_attn = out_weight[0]
    w_router = router_weight[0]
    hidden_local = expert_out.shape[2]
    w_inner = expert_in[0].reshape(EXPERTS, 2 * hidden_local, width)
    w_outer = expert_out[0]
    token_pos = (
        seq_index * rows
        + window_attention_index * part_rows
        + jnp.arange(part_rows, dtype=jnp.int32)
    )
    head_index = jnp.arange(head_rows, dtype=jnp.int32)
    query_pos = (
        head_index // part_rows * rows + window_attention_index * part_rows + head_index % part_rows
    )
    key_index = jnp.arange(length, dtype=jnp.int32)
    key_pos = (
        key_index % head_rows // part_rows * rows
        + key_index // head_rows * part_rows
        + key_index % part_rows
    )
    causal = key_pos[None, :] <= query_pos[:, None]
    token_cos, token_sin = rotary_angles(token_pos, HEAD_DIM)
    query_cos, query_sin = rotary_angles(query_pos, HEAD_DIM)

    def feature_total(values):
        return lax.psum(values, "wa")

    def token_sum(left, apply):
        return lax.psum_scatter(
            apply(left).astype(jnp.bfloat16), "wa", scatter_dimension=0, tiled=True
        ).astype(jnp.float32)

    def to_heads(values):
        return lax.all_to_all(values, "seq", split_axis=1, concat_axis=0, tiled=True)

    def to_tokens(values):
        return lax.all_to_all(values, "seq", split_axis=0, concat_axis=1, tiled=True)

    def to_rows(values):
        return lax.all_gather(values, "wa", axis=0, tiled=True)

    def features(values):
        return lax.all_gather(values, "wa", axis=1, tiled=True)

    def feature_share(values):
        return lax.psum_scatter(
            values.astype(jnp.bfloat16), "wa", scatter_dimension=1, tiled=True
        ).astype(jnp.float32)

    def normalize(values, gain):
        total = feature_total(jnp.sum(values * values, axis=1))
        scale = lax.rsqrt(total / width + epsilon)
        return (scale, (values * scale[:, None] * gain).astype(jnp.bfloat16))

    def norm_back(grad, values, scale, gain):
        scaled = grad * gain
        total = feature_total(jnp.sum(values * scaled, axis=1))
        input_grad = (
            scale[:, None] * scaled - values * (scale * scale * scale * total / width)[:, None]
        )
        return (input_grad, jnp.sum(grad * values * scale[:, None], axis=0))

    def attention_scores(queries, keys):
        scores = (
            jnp.einsum("qghd,kgd->ghqk", queries, keys, preferred_element_type=jnp.float32)
            * attention_score_scale
        )
        return jnp.where(causal[None, None], scores, -1e30)

    received = jnp.zeros((rows, width_local), jnp.bfloat16)
    saved_residuals = []
    sent_list = []
    for clock_step_index in range(microbatch + 1):
        own_input = first_layer_input[min(clock_step_index, microbatch - 1)].T
        layer_in = jnp.where(section_first, own_input, received)
        route_ids = jnp.where(
            section_first,
            routes[0, min(clock_step_index, microbatch - 1)],
            routes[0, max(clock_step_index - 1, 0)],
        )
        forward_resid = layer_in.astype(jnp.float32)
        forward_scale_one, forward_normed_one = normalize(forward_resid, gain_one)
        qkv_sum = token_sum(
            forward_normed_one,
            lambda piece: jnp.dot(piece, w_qkv, preferred_element_type=jnp.float32),
        )
        grouped = qkv_sum.reshape(part_rows, KV_HEADS, per_group + 2, HEAD_DIM)
        turned = rotate(
            grouped[:, :, : per_group + 1].reshape(part_rows, -1, HEAD_DIM), token_cos, token_sin
        )
        turned = jnp.concatenate(
            [
                turned.reshape(part_rows, KV_HEADS, per_group + 1, HEAD_DIM),
                grouped[:, :, per_group + 1 :],
            ],
            axis=2,
        )
        heads = to_heads(turned.reshape(part_rows, -1).astype(jnp.bfloat16))
        heads = heads.reshape(head_rows, group_count, per_group + 2, HEAD_DIM)
        forward_queries = heads[:, :, :per_group]
        forward_key_value = lax.all_gather(
            heads[:, :, per_group:].reshape(head_rows, -1), "wa", axis=0, tiled=True
        )
        forward_key_value = forward_key_value.reshape(length, group_count, 2, HEAD_DIM)
        forward_scores = attention_scores(forward_queries, forward_key_value[:, :, 0])
        top_score = jnp.max(forward_scores, axis=3, keepdims=True)
        raised = jnp.exp(forward_scores - top_score)
        forward_total = jnp.sum(raised, axis=3, keepdims=True)
        forward_probs = (raised / forward_total).astype(jnp.bfloat16)
        forward_log_total = top_score + jnp.log(forward_total)
        mixed = jnp.einsum(
            "ghqk,kgd->qghd",
            forward_probs,
            forward_key_value[:, :, 1],
            preferred_element_type=jnp.float32,
        )
        forward_gathered_out = to_rows(to_tokens(mixed.reshape(head_rows, -1).astype(jnp.bfloat16)))
        forward_middle = forward_resid + lax.dot_general(
            forward_gathered_out,
            w_attn,
            (((1,), (1,)), ((), ())),
            preferred_element_type=jnp.float32,
        )
        forward_scale_two, forward_normed_two = normalize(forward_middle, gain_two)
        forward_full_normed = features(forward_normed_two)
        logits = feature_total(
            jnp.dot(forward_normed_two, w_router, preferred_element_type=jnp.float32)
        )
        forward_gates = jax.nn.softmax(jnp.take_along_axis(logits, route_ids, axis=1), axis=1)
        forward_slots, forward_owner = slot_table(route_ids, capacity)
        forward_padded = jnp.concatenate(
            [forward_full_normed, jnp.zeros((1, width), jnp.bfloat16)], axis=0
        )
        forward_expert_rows = forward_padded[forward_owner].reshape(EXPERTS, capacity, width)
        forward_gate_up = jnp.einsum(
            "ecd,ehd->ech", forward_expert_rows, w_inner, preferred_element_type=jnp.float32
        )
        forward_active = (
            jax.nn.silu(forward_gate_up[..., :hidden_local]) * forward_gate_up[..., hidden_local:]
        ).astype(jnp.bfloat16)
        results = jnp.einsum(
            "ech,ehd->ecd", forward_active, w_outer, preferred_element_type=jnp.float32
        ).reshape(-1, width)
        picked = results[forward_slots].reshape(rows, TOP, width)
        output = forward_middle + feature_share(jnp.sum(forward_gates[:, :, None] * picked, axis=1))
        forward_saved_residual = (
            forward_resid,
            forward_scale_one,
            forward_normed_one,
            forward_queries,
            forward_key_value,
            forward_log_total,
            forward_gathered_out,
            forward_middle,
            forward_scale_two,
            forward_normed_two,
            forward_full_normed,
            forward_gates,
            forward_slots,
            forward_owner,
            forward_gate_up,
            forward_active,
        )
        output, saved_residual = (output, forward_saved_residual)
        sent = output.astype(jnp.bfloat16)
        sent_list.append(sent)
        if clock_step_index < microbatch:
            received = passed_along(sent, "section", 1)
        saved_residuals.append(saved_residual)
    back_received = jnp.zeros((rows, width_local), jnp.bfloat16)
    grad_list = []
    small_total = None
    large_total = None
    for clock_step_index in range(microbatch + 1):
        if clock_step_index < microbatch:
            own_grad = cotangent[clock_step_index].T.astype(jnp.float32)
        else:
            own_grad = jnp.zeros((rows, width_local), jnp.float32)
        grad_in = jnp.where(section_first, back_received.astype(jnp.float32), own_grad)
        saved = jax.tree.map(
            lambda early, late: jnp.where(section_first, early, late),
            saved_residuals[max(clock_step_index - 1, 0)],
            saved_residuals[min(clock_step_index + 1, microbatch)],
        )
        (
            resid,
            scale_one,
            normed_one,
            backward_queries,
            key_value,
            log_total,
            gathered_out,
            middle,
            scale_two,
            normed_two,
            full_normed,
            gates,
            slots,
            owner,
            gate_up,
            active,
        ) = saved
        backward_keys = key_value[:, :, 0]
        backward_values = key_value[:, :, 1]
        moe_full = features(grad_in.astype(jnp.bfloat16))
        padded_grad = jnp.concatenate([moe_full, jnp.zeros((1, width), jnp.bfloat16)], axis=0)
        slot_grad = padded_grad[owner].reshape(EXPERTS, capacity, width)
        slot_gate = (
            jnp.zeros((EXPERTS * capacity,), jnp.float32)
            .at[slots]
            .set(gates.reshape(-1))
            .reshape(EXPERTS, capacity, 1)
        )
        through = jnp.einsum("ecd,ehd->ech", slot_grad, w_outer, preferred_element_type=jnp.float32)
        slot_dot = jnp.sum(active.astype(jnp.float32) * through, axis=2).reshape(-1)
        gate_grad = feature_total(slot_dot[slots].reshape(rows, TOP))
        result_grad = (slot_gate * slot_grad).astype(jnp.bfloat16)
        active_grad = jnp.einsum(
            "ecd,ehd->ech", result_grad, w_outer, preferred_element_type=jnp.float32
        )
        outer_grad = jnp.einsum(
            "ech,ecd->ehd", active, result_grad, preferred_element_type=jnp.float32
        )
        gate_part = gate_up[..., :hidden_local]
        up_part = gate_up[..., hidden_local:]
        sigmoid = jax.nn.sigmoid(gate_part)
        gate_up_grad = jnp.concatenate(
            [
                active_grad * up_part * sigmoid * (1.0 + gate_part * (1.0 - sigmoid)),
                active_grad * gate_part * sigmoid,
            ],
            axis=-1,
        ).astype(jnp.bfloat16)
        padded = jnp.concatenate([full_normed, jnp.zeros((1, width), jnp.bfloat16)], axis=0)
        expert_rows = padded[owner].reshape(EXPERTS, capacity, width)
        inner_grad = jnp.einsum(
            "ech,ecd->ehd", gate_up_grad, expert_rows, preferred_element_type=jnp.float32
        )
        row_grad = jnp.einsum(
            "ech,ehd->ecd", gate_up_grad, w_inner, preferred_element_type=jnp.float32
        ).reshape(-1, width)
        token_grad = jnp.sum(row_grad[slots].reshape(rows, TOP, width), axis=1)
        chosen_grad = gates * (gate_grad - jnp.sum(gates * gate_grad, axis=1, keepdims=True))
        expert_ids = (slots // capacity).reshape(rows, TOP)
        selector = (
            expert_ids[:, :, None] == jnp.arange(EXPERTS, dtype=jnp.int32)[None, None, :]
        ).astype(jnp.float32)
        logit_grad = jnp.sum(chosen_grad[:, :, None] * selector, axis=1)
        router_grad = jnp.dot(
            normed_two.astype(jnp.float32).T, logit_grad, precision=lax.Precision.HIGHEST
        )
        normed_grad = feature_share(token_grad) + jnp.dot(
            logit_grad, w_router.astype(jnp.float32).T, precision=lax.Precision.HIGHEST
        )
        input_two, gain_two_grad = norm_back(normed_grad, middle, scale_two, gain_two)
        middle_grad = grad_in + input_two
        attn_grad = middle_grad.astype(jnp.bfloat16)
        attn_weight_grad = lax.dot_general(
            attn_grad, gathered_out, (((0,), (0,)), ((), ())), preferred_element_type=jnp.float32
        )
        mixed_grad = token_sum(
            attn_grad, lambda piece: jnp.dot(piece, w_attn, preferred_element_type=jnp.float32)
        )
        out_heads = to_heads(mixed_grad.astype(jnp.bfloat16)).reshape(
            head_rows, group_count, per_group, HEAD_DIM
        )
        probs = jnp.exp(attention_scores(backward_queries, backward_keys) - log_total)
        value_grad = jnp.einsum(
            "ghqk,qghd->kgd",
            probs.astype(jnp.bfloat16),
            out_heads,
            preferred_element_type=jnp.float32,
        )
        prob_grad = jnp.einsum(
            "qghd,kgd->ghqk", out_heads, backward_values, preferred_element_type=jnp.float32
        )
        score_grad = (
            probs * (prob_grad - jnp.sum(probs * prob_grad, axis=3, keepdims=True))
        ).astype(jnp.bfloat16)
        query_grad = (
            jnp.einsum(
                "ghqk,kgd->qghd", score_grad, backward_keys, preferred_element_type=jnp.float32
            )
            * attention_score_scale
        )
        key_grad = (
            jnp.einsum(
                "ghqk,qghd->kgd", score_grad, backward_queries, preferred_element_type=jnp.float32
            )
            * attention_score_scale
        )
        pair_grad = lax.psum_scatter(
            jnp.stack([key_grad, value_grad], axis=2).reshape(length, -1).astype(jnp.bfloat16),
            "wa",
            scatter_dimension=0,
            tiled=True,
        ).astype(jnp.float32)
        pair_grad = pair_grad.reshape(head_rows, group_count, 2, HEAD_DIM)
        query_back = rotate(query_grad.reshape(head_rows, -1, HEAD_DIM), query_cos, -query_sin)
        query_back = query_back.reshape(head_rows, group_count, per_group, HEAD_DIM)
        key_back = rotate(pair_grad[:, :, 0], query_cos, -query_sin)
        head_grads = jnp.concatenate(
            [query_back, key_back[:, :, None], pair_grad[:, :, 1:]], axis=2
        )
        full_grads = to_rows(to_tokens(head_grads.reshape(head_rows, -1).astype(jnp.bfloat16)))
        normed_one_grad = lax.dot_general(
            full_grads, w_qkv, (((1,), (1,)), ((), ())), preferred_element_type=jnp.float32
        )
        qkv_grad = lax.dot_general(
            normed_one, full_grads, (((0,), (0,)), ((), ())), preferred_element_type=jnp.float32
        )
        input_one, gain_one_grad = norm_back(normed_one_grad, resid, scale_one, gain_one)
        grads = (
            jnp.stack([gain_one_grad, gain_two_grad]),
            qkv_grad,
            attn_weight_grad,
            router_grad,
            inner_grad.reshape(EXPERTS, 2, hidden_local, width),
            outer_grad,
        )
        layer_grad, grads = (middle_grad + input_one, grads)
        grad_list.append(layer_grad)
        if clock_step_index < microbatch:
            back_received = passed_along(layer_grad.astype(jnp.bfloat16), "section", -1)
        small_part = (grads[0], grads[3])
        large_part = (grads[1], grads[2], grads[4], grads[5])
        if small_total is None:
            small_total = small_part
            large_total = large_part
        else:
            small_total = jax.tree.map(lambda older, newer: older + newer, small_total, small_part)
            large_total = jax.tree.map(lambda older, newer: older + newer, large_total, large_part)
    large_total = (
        lax.psum_scatter(
            large_total[0].astype(jnp.bfloat16), "seq", scatter_dimension=1, tiled=True
        ).astype(jnp.float32),
        lax.psum_scatter(
            large_total[1].astype(jnp.bfloat16), "seq", scatter_dimension=1, tiled=True
        ).astype(jnp.float32),
        lax.psum_scatter(
            large_total[2].astype(jnp.bfloat16), "seq", scatter_dimension=3, tiled=True
        ).astype(jnp.float32),
        lax.psum_scatter(
            large_total[3].astype(jnp.bfloat16), "seq", scatter_dimension=2, tiled=True
        ).astype(jnp.float32),
    )
    small_total = lax.psum(small_total, "seq")
    layer_outputs = jnp.stack(
        [
            jnp.where(section_first, sent_list[index], sent_list[index + 1])
            for index in range(microbatch)
        ]
    )
    input_grads = jnp.stack(
        [
            jnp.where(section_first, grad_list[index + 1], grad_list[index])
            for index in range(microbatch)
        ]
    )
    return (
        layer_outputs[None],
        input_grads[None],
        small_total[0][None],
        large_total[0][None],
        large_total[1][None],
        small_total[1][None],
        large_total[2][None],
        large_total[3][None],
    )


def solution(mesh):
    return jax.shard_map(
        on_device,
        mesh=mesh,
        in_specs=(
            P(None, "wa", "seq"),
            P("section", None, "seq", None),
            P(None, "wa", "seq"),
            P("section", None, "wa"),
            P("section", "wa", None),
            P("section", "wa", None),
            P("section", "wa", None),
            P("section", None, None, "wa", None),
            P("section", None, "wa", None),
        ),
        out_specs=(
            P("section", None, "seq", "wa"),
            P("section", None, "seq", "wa"),
            P("section", None, "wa"),
            P("section", "wa", "seq"),
            P("section", "wa", "seq"),
            P("section", "wa", None),
            P("section", None, None, "wa", "seq"),
            P("section", None, "wa", "seq"),
        ),
        check_vma=False,
    )
```

profile of v0, /device:TPU:1, one launch (start us, length us, event | category | flops | bytes accessed | tf_op | source)
XLA Modules:
  0.0 1825.3 jit_solution(7702349285060861940)
XLA Ops:
  8.2 13.2 psum.140
  26.2 11.3 reduce-window.20
  37.5 11.2 reduce-window.26
  48.7 11.3 reduce-window.24
  94.4 15.6 all_gather.45
  122.1 14.1 all_gather.46
  136.6 11.9 psum.141
  148.7 13.8 all_gather.47
  162.6 20.7 %psum.142 = f32[128,40]{0,1:T(8,128)S(1)} all-reduce(f32[128,40]{0,1:T(8,128)S(1)} %fusion.207), channel_id=1, replica_groups=mesh['section'=2,'seq'=8,'wa'=8] {'wa'}, use_global_device_ids=true, to_apply=%region_7.8 | all-reduce | flops 5120 | bytes 40960 | tf_op jit(solution)/shard_map/psum | solution.py:106
  196.4 11.8 fusion.324
  215.9 11.1 gather_fusion.1
  233.1 26.1 %reduce-scatter.36.cloned.1.call-done = bf16[128,192]{0,1:T(8,128)(2,1)} async-done(((bf16[128,1536]{0,1:T(8,128)(2,1)}), bf16[128,192]{0,1:T(8,128)(2,1)}) %reduce-scatter.36.cloned.1.call-update) | async-done | bytes 49168 | tf_op jit(solution)/shard_map/reduce_scatter | solution.py:126
  264.6 15.8 psum.143
  282.1 13.5 all_gather.54
  297.4 12.6 reduce-scatter.38.cloned.1.call-done
  334.9 16.3 all_gather.48
  371.7 13.0 all_gather.49
  385.8 11.9 psum.144
  399.8 13.8 all_gather.50
  421.7 12.9 broadcast_select_fusion.8
  455.8 20.7 %all-reduce.12 = (f32[128,40]{0,1:T(8,128)S(1)}, f32[128,8]{0,1:T(8,128)S(1)}) all-reduce(f32[128,40]{0,1:T(8,128)S(1)} %copy-done.113, f32[128,8]{0,1:T(8,128)S(1)} %copy.447), channel_id=1, replica_groups=mesh['section'=2,'seq'=8,'wa'=8] {'wa'}, use_global_device_ids=true, to_apply=%region_23.25 | all-reduce | flops 6144 | bytes 49152 | tf_op jit(solution)/shard_map/psum | solution.py:106
  489.8 11.1 gather_fusion.3
  513.9 11.1 fusion.187
  525.0 11.1 gather_fusion.7
  547.3 24.2 %reduce-scatter.46.cloned.1.call-done = bf16[128,192]{0,1:T(8,128)(2,1)} async-done(((bf16[128,1536]{0,1:T(8,128)(2,1)}), bf16[128,192]{0,1:T(8,128)(2,1)}) %reduce-scatter.46.cloned.1.call-update) | async-done | bytes 49168 | tf_op jit(solution)/shard_map/reduce_scatter | solution.py:126
  573.3 15.1 all-reduce.11
  595.3 23.2 %reduce-scatter.48.cloned.1.call-done = bf16[16,1536]{1,0:T(8,128)(2,1)} async-done(((bf16[128,1536]{1,0:T(8,128)(2,1)}), bf16[16,1536]{1,0:T(8,128)(2,1)}) %reduce-scatter.48.cloned.1.call-update) | async-done | bytes 49168 | tf_op jit(solution)/shard_map/reduce_scatter | solution.py:109
  626.8 25.0 %reduce-scatter.42.cloned.1.call-done = bf16[16,2560]{1,0:T(8,128)(2,1)} async-done(((bf16[128,2560]{1,0:T(8,128)(2,1)}), bf16[16,2560]{1,0:T(8,128)(2,1)}) %reduce-scatter.42.cloned.1.call-update) | async-done | bytes 81936 | tf_op jit(solution)/shard_map/reduce_scatter | solution.py:109
  670.1 16.5 all_gather.51
  710.0 14.4 all_gather.52
  743.5 16.8 all_gather.55
  763.4 11.9 all-reduce.10
  780.3 13.9 all_gather.53
  802.5 13.2 broadcast_select_fusion.6
  818.2 13.2 all_gather.56
  851.9 20.4 %all-reduce.9 = (f32[128,40]{0,1:T(8,128)S(1)}, f32[128,8]{0,1:T(8,128)S(1)}) all-reduce(f32[128,40]{0,1:T(8,128)S(1)} %fusion.203, f32[128,8]{0,1:T(8,128)S(1)} %copy.460), channel_id=1, replica_groups=mesh['section'=2,'seq'=8,'wa'=8] {'wa'}, use_global_device_ids=true, to_apply=%region_39.41 | all-reduce | flops 6144 | bytes 49152 | tf_op jit(solution)/shard_map/psum | solution.py:106
  903.0 11.1 gather_fusion.10
  919.7 28.0 %reduce-scatter.50.cloned.1.call-done = bf16[128,192]{0,1:T(8,128)(2,1)} async-done(((bf16[128,1536]{0,1:T(8,128)(2,1)}), bf16[128,192]{0,1:T(8,128)(2,1)}) %reduce-scatter.50.cloned.1.call-update) | async-done | bytes 49168 | tf_op jit(solution)/shard_map/reduce_scatter | solution.py:126
  949.5 15.1 psum.153
  966.7 27.4 %reduce-scatter.52.cloned.1.call-done = bf16[16,1536]{1,0:T(8,128)(2,1)} async-done(((bf16[128,1536]{1,0:T(8,128)(2,1)}), bf16[16,1536]{1,0:T(8,128)(2,1)}) %reduce-scatter.52.cloned.1.call-update) | async-done | bytes 49168 | tf_op jit(solution)/shard_map/reduce_scatter | solution.py:109
  995.0 13.1 all_to_all.183
  1013.6 25.2 %reduce-scatter.60.cloned.1.call-done = bf16[128,128]{1,0:T(8,128)(2,1)} async-done(((bf16[1024,128]{1,0:T(8,128)(2,1)}), bf16[128,128]{1,0:T(8,128)(2,1)}) %reduce-scatter.60.cloned.1.call-update) | async-done | bytes 32784
  1054.4 17.8 all_gather.57
  1074.1 11.9 psum.154
  1092.2 15.0 all_gather.58
  1128.1 11.9 psum.155
  1152.7 11.0 fusion.183
  1163.7 11.1 gather_fusion.13
  1182.0 23.2 %reduce-scatter.54.cloned.1.call-done = bf16[128,192]{0,1:T(8,128)(2,1)} async-done(((bf16[128,1536]{0,1:T(8,128)(2,1)}), bf16[128,192]{0,1:T(8,128)(2,1)}) %reduce-scatter.54.cloned.1.call-update) | async-done | bytes 49168 | tf_op jit(solution)/shard_map/reduce_scatter | solution.py:126
  1207.5 15.1 psum.156
  1237.8 15.6 reduce-scatter.56.cloned.1.call-done
  1283.3 11.0 gather_fusion.5
  1324.8 19.1 %all_gather.59 = bf16[128,2560]{1,0:T(8,128)(2,1)S(1)} all-gather(bf16[16,2560]{1,0:T(8,128)(2,1)S(1)} %all_to_all.170), channel_id=1, replica_groups=mesh['section'=2,'seq'=8,'wa'=8] {'wa'}, dimensions={0}, use_global_device_ids=true | all-gather | bytes 737280 | tf_op jit(solution)/shard_map/all_gather | solution.py:120
  1360.1 16.0 add_convert_fusion.1
  1376.1 17.9 copy.514
  1394.0 20.7 %reshape.1704 = bf16[1536,2560]{1,0:T(8,128)(2,1)} reshape(bf16[1536,40,64]{2,1,0:T(8,128)(2,1)} %bitcast.852) | data formatting | bytes 15728640
  1433.1 17.5 fusion.186
  1450.7 12.5 fusion.184
  1463.2 28.1 %add_convert_fusion = bf16[40,128,1536]{2,1,0:T(8,128)(2,1)} fusion(f32[40,128,1536]{2,1,0:T(8,128)} %fusion.186, f32[40,128,1536]{2,1,0:T(8,128)} %fusion.184, bf16[40,32,1536]{2,1,0:T(8,128)(2,1)S(1)} %bitcast.866, bf16[40,32,64]{2,1,0:T(8,128)(2,1)} %copy-done.55, bf16[40,32,64]{2,1,0:T(8,128)(2,1)} %copy-done.54), kind=kOutput, calls=%fused_computation.27 | convolution fusion | flops 527564800 | bytes 82903040 | tf_op jit(solution)/shard_map/ech,ecd->ehd/dot_general | solution.py:316
  1491.3 62.7 %copy.512 = bf16[40,2,64,1536]{2,1,0,3:T(2,128)(2,1)} copy(bf16[40,2,64,1536]{3,2,1,0:T(8,128)(2,1)} %bitcast.851) | data formatting | bytes 31457280
  1554.0 64.5 %reshape.1702 = bf16[1536,5120]{1,0:T(8,128)(2,1)} reshape(bf16[1536,40,2,64]{3,2,1,0:T(2,128)(2,1)} %bitcast.850) | data formatting | bytes 31457280
  1623.8 12.4 psum.157
  1636.3 33.3 %all-reduce.13 = (f32[1,2,192]{2,1,0:T(2,128)}, f32[1,192,40]{1,2,0:T(8,128)}) all-reduce(f32[1,2,192]{2,1,0:T(2,128)S(1)} %fusion.282, f32[1,192,40]{1,2,0:T(8,128)S(1)} %fusion.82), channel_id=1, replica_groups=mesh['section'=2,'seq'=8,'wa'=8] {'seq'}, use_global_device_ids=true, to_apply=%region_96.98 | all-reduce | flops 8064 | bytes 64512 | tf_op jit(solution)/shard_map/psum | solution.py:427
  1681.1 114.1 %reduce-scatter.68.cloned.1.call-done = bf16[192,5120]{1,0:T(8,128)(2,1)} async-done(((bf16[1536,5120]{1,0:T(8,128)(2,1)}), bf16[192,5120]{1,0:T(8,128)(2,1)}) %reduce-scatter.68.cloned.1.call-update) | async-done | bytes 1966096
  (853 shorter events, 581.8 us)
Async XLA Ops:
  7.2 69.8 %reduce-scatter.34.cloned.1.call-start = ((), (), s32[]{:S(2)}) async-start(), calls=%async_computation.31 | async-start | bytes 737280 | tf_op jit(solution)/shard_map/reduce_scatter | solution.py:109
  22.1 566.9 %copy-start.105 = (f32[1,1,192]{2,1,0:T(1,128)}, f32[1,1,192]{2,1,0:T(1,128)S(1)}, u32[]{:S(2)}) copy-start(f32[1,1,192]{2,1,0:T(1,128)S(1)} %get-tuple-element.116) | copy-start | bytes 2308
  22.1 1063.9 %copy-start.98 = (f32[1,1,192]{2,1,0:T(1,128)}, f32[1,1,192]{2,1,0:T(1,128)S(1)}, u32[]{:S(2)}) copy-start(f32[1,1,192]{2,1,0:T(1,128)S(1)} %get-tuple-element.117) | copy-start | bytes 2308
  76.1 237.8 %copy-start.101 = (f32[16,32]{1,0:T(8,128)}, f32[16,32]{1,0:T(8,128)S(1)}, u32[]{:S(2)}) copy-start(f32[16,32]{1,0:T(8,128)S(1)} %get-tuple-element.120) | copy-start | bytes 6148
  77.0 931.7 %copy-start.38 = (pred[128,1024]{0,1:T(8,128)(4,1)}, pred[128,1024]{0,1:T(8,128)(4,1)S(1)}, u32[]{:S(2)}) copy-start(pred[128,1024]{0,1:T(8,128)(4,1)S(1)} %broadcast_compare_fusion) | copy-start | bytes 393220
  79.6 14.3 all-to-all-start
  112.1 9.9 all-to-all-start.1
  115.4 143.8 %reduce-scatter.36.cloned.1.call-start = ((), (), s32[]{:S(2)}) async-start(), calls=%async_computation.32 | async-start | bytes 442368 | tf_op jit(solution)/shard_map/reduce_scatter | solution.py:126
  232.1 63.4 %copy-start.148 = (s32[1024,1]{0,1:T(1,128)S(1)}, s32[1024,1]{0,1:T(1,128)}, u32[]{:S(2)}) copy-start(s32[1024,1]{0,1:T(1,128)} %copy-done.147) | copy-start | bytes 12292
  232.1 64.6 %copy-start.146 = (s32[1024,1]{0,1:T(1,128)S(1)}, s32[1024,1]{0,1:T(1,128)}, u32[]{:S(2)}) copy-start(s32[1024,1]{0,1:T(1,128)} %get-tuple-element.98) | copy-start | bytes 12292
  232.1 81.8 %copy-start.104 = (f32[16,32]{1,0:T(8,128)S(1)}, f32[16,32]{1,0:T(8,128)}, u32[]{:S(2)}) copy-start(f32[16,32]{1,0:T(8,128)} %copy-done.103) | copy-start | bytes 6148
  233.1 90.5 %copy-start.140 = (s32[1280]{0:T(1024)S(1)}, s32[1280]{0:T(1024)}, u32[]{:S(2)}) copy-start(s32[1280]{0:T(1024)} %get-tuple-element.103) | copy-start | bytes 15364
  233.1 76.9 %reduce-scatter.38.cloned.1.call-start = ((), (), s32[]{:S(2)}) async-start(), calls=%async_computation.33 | async-start | bytes 737280 | tf_op jit(solution)/shard_map/reduce_scatter | solution.py:109
  260.1 4.5 collective-permute-start
  264.6 512.6 %copy-start.15 = (bf16[128,192]{0,1:T(8,128)(2,1)}, bf16[128,192]{0,1:T(8,128)(2,1)S(1)}, u32[]{:S(2)}) copy-start(bf16[128,192]{0,1:T(8,128)(2,1)S(1)} %get-tuple-element.53) | copy-start | bytes 147460
  282.0 69.6 %copy-start.129 = (s32[128,8]{0,1:T(8,128)}, s32[128,8]{0,1:T(8,128)S(1)}, u32[]{:S(2)}) copy-start(s32[128,8]{0,1:T(8,128)S(1)} %copy.446) | copy-start | bytes 12292
  282.1 69.8 %copy-start.131 = (s32[128,8]{0,1:T(8,128)}, s32[128,8]{0,1:T(8,128)S(1)}, u32[]{:S(2)}) copy-start(s32[128,8]{0,1:T(8,128)S(1)} %copy.459) | copy-start | bytes 12292
  316.9 13.3 all-to-all-start.2
  354.7 15.4 all-to-all-start.3
  358.1 185.4 %reduce-scatter.40.cloned.1.call-start = ((), (), s32[]{:S(2)}) async-start(), calls=%async_computation.34 | async-start | bytes 442368 | tf_op jit(solution)/shard_map/reduce_scatter | solution.py:126
  385.8 185.7 %copy-start.35 = (f32[128,192]{0,1:T(8,128)}, f32[128,192]{0,1:T(8,128)S(1)}, u32[]{:S(2)}) copy-start(f32[128,192]{0,1:T(8,128)S(1)} %get-tuple-element.138) | copy-start | bytes 294916
  506.9 64.6 %reduce-scatter.46.cloned.1.call-start = ((), (), s32[]{:S(2)}) async-start(), calls=%async_computation.37 | async-start | bytes 442368 | tf_op jit(solution)/shard_map/reduce_scatter | solution.py:126
  540.4 112.6 %copy-start.102 = (f32[16,32]{1,0:T(8,128)S(1)}, f32[16,32]{1,0:T(8,128)}, u32[]{:S(2)}) copy-start(f32[16,32]{1,0:T(8,128)} %copy-done.101) | copy-start | bytes 6148
  541.4 77.0 %reduce-scatter.48.cloned.1.call-start = ((), (), s32[]{:S(2)}) async-start(), calls=%async_computation.38 | async-start | bytes 442368 | tf_op jit(solution)/shard_map/reduce_scatter | solution.py:109
  543.5 83.3 %copy-start.92 = (f32[128,40]{0,1:T(8,128)}, f32[128,40]{0,1:T(8,128)S(1)}, u32[]{:S(2)}) copy-start(f32[128,40]{0,1:T(8,128)S(1)} %select_reduce_fusion.2) | copy-start | bytes 61444
  545.0 81.8 %copy-start.89 = (bf16[128,192]{0,1:T(8,128)(2,1)}, bf16[128,192]{0,1:T(8,128)(2,1)S(1)}, u32[]{:S(2)}) copy-start(bf16[128,192]{0,1:T(8,128)(2,1)S(1)} %get-tuple-element.43) | copy-start | bytes 147460
  545.0 28.3 %collective-permute-start.1 = (bf16[128,192]{0,1:T(8,128)(2,1)S(1)}, bf16[128,192]{0,1:T(8,128)(2,1)S(1)}, u32[]{:S(2)}, u32[]{:S(2)}) collective-permute-start(bf16[128,192]{0,1:T(8,128)(2,1)S(1)} %get-tuple-element.43), channel_id=1, source_target_pairs={{0,64},{1,65},{2,66},{3,67},{4,68},{5,69},{6,70},{7,71},{8,72},{9,... | collective-permute-start | bytes 147464 | tf_op jit(solution)/shard_map/ppermute | solution.py:19
  573.3 770.7 %copy-start.13 = (bf16[128,192]{0,1:T(8,128)(2,1)}, bf16[128,192]{0,1:T(8,128)(2,1)S(1)}, u32[]{:S(2)}) copy-start(bf16[128,192]{0,1:T(8,128)(2,1)S(1)} %get-tuple-element.51) | copy-start | bytes 147460
  589.9 65.2 %copy-start.41 = (f32[128,192]{0,1:T(8,128)}, f32[128,192]{0,1:T(8,128)S(1)}, u32[]{:S(2)}) copy-start(f32[128,192]{0,1:T(8,128)S(1)} %bitcast_add_fusion) | copy-start | bytes 294916
  591.0 60.8 %reduce-scatter.42.cloned.1.call-start = ((), (), s32[]{:S(2)}) async-start(), calls=%async_computation.35 | async-start | bytes 737280 | tf_op jit(solution)/shard_map/reduce_scatter | solution.py:109
  593.9 95.0 %copy-start.157 = (f32[128]{0:T(128)}, f32[128]{0:T(128)S(1)}, u32[]{:S(2)}) copy-start(f32[128]{0:T(128)S(1)} %fusion.304) | copy-start | bytes 1540
  595.2 107.5 %copy-start.83 = (f32[128,32]{0,1:T(8,128)}, f32[128,32]{0,1:T(8,128)S(1)}, u32[]{:S(2)}) copy-start(f32[128,32]{0,1:T(8,128)S(1)} %get-tuple-element.119) | copy-start | bytes 49156
  620.0 35.1 %all-to-all-start.6 = ((bf16[16,8,192]{2,0,1:T(8,128)(2,1)}), bf16[16,8,192]{2,0,1:T(8,128)(2,1)}, u32[]{:S(2)}, u32[]{:S(2)}) async-start(bf16[16,8,192]{2,0,1:T(8,128)(2,1)} %copy.448), calls=%async_computation.14 | async-start | bytes 131072 | tf_op jit(solution)/shard_map/all_to_all | solution.py:114
  655.1 13.0 all-to-all-start.4
  661.4 63.0 %reduce-scatter.58.cloned.1.call-start = ((), (), s32[]{:S(2)}) async-start(), calls=%async_computation.43 | async-start | bytes 294912
  696.2 84.0 %copy-start.106 = (f32[1,1,192]{2,1,0:T(1,128)S(1)}, f32[1,1,192]{2,1,0:T(1,128)}, u32[]{:S(2)}) copy-start(f32[1,1,192]{2,1,0:T(1,128)} %copy-done.105) | copy-start | bytes 2308
  699.3 9.9 all-to-all-start.5
  724.4 55.8 %copy-start.28 = (bf16[128,1536]{1,0:T(8,128)(2,1)}, bf16[128,1536]{1,0:T(8,128)(2,1)S(1)}, u32[]{:S(2)}) copy-start(bf16[128,1536]{1,0:T(8,128)(2,1)S(1)} %all_gather.52) | copy-start | bytes 1179652
  729.6 10.7 all-to-all-start.7
  733.6 214.2 %reduce-scatter.50.cloned.1.call-start = ((), (), s32[]{:S(2)}) async-start(), calls=%async_computation.39 | async-start | bytes 442368 | tf_op jit(solution)/shard_map/reduce_scatter | solution.py:126
  734.0 213.8 %copy-start.36 = (f32[128,192]{0,1:T(8,128)}, f32[128,192]{0,1:T(8,128)S(1)}, u32[]{:S(2)}) copy-start(f32[128,192]{0,1:T(8,128)S(1)} %get-tuple-element.145) | copy-start | bytes 294916
  778.9 38.5 %collective-permute-start.2 = (bf16[128,192]{0,1:T(8,128)(2,1)}, bf16[128,192]{0,1:T(8,128)(2,1)}, u32[]{:S(2)}, u32[]{:S(2)}) collective-permute-start(bf16[128,192]{0,1:T(8,128)(2,1)} %get-tuple-element.44), channel_id=1, source_target_pairs={{64,0},{65,1},{66,2},{67,3},{68,4},{69,5},{70,6},{71,7},{72,8},{73... | collective-permute-start | bytes 147464 | tf_op jit(solution)/shard_map/ppermute | solution.py:19
  914.1 94.2 %copy-start.40 = (bf16[1024,1,2,64]{0,3,2,1:T(8,128)(2,1)S(1)}, bf16[1024,1,2,64]{0,3,2,1:T(8,128)(2,1)}, u32[]{:S(2)}) copy-start(bf16[1024,1,2,64]{0,3,2,1:T(8,128)(2,1)} %get-tuple-element.72) | copy-start | bytes 786436
  918.4 90.3 %copy-start.61 = (bf16[128,1,3,64]{0,3,2,1:T(8,128)(2,1)S(1)}, bf16[128,1,3,64]{0,3,2,1:T(8,128)(2,1)}, u32[]{:S(2)}) copy-start(bf16[128,1,3,64]{0,3,2,1:T(8,128)(2,1)} %copy-done.59) | copy-start | bytes 147460
  918.5 90.3 %copy-start.171 = (f32[3,128]{1,0:T(4,128)S(1)}, f32[3,128]{1,0:T(4,128)}, u32[]{:S(2)}) copy-start(f32[3,128]{1,0:T(4,128)} %get-tuple-element.114) | copy-start | bytes 4612
  919.4 89.3 %copy-start.63 = (bf16[128,1,3,64]{0,3,2,1:T(8,128)(2,1)S(1)}, bf16[128,1,3,64]{0,3,2,1:T(8,128)(2,1)}, u32[]{:S(2)}) copy-start(bf16[128,1,3,64]{0,3,2,1:T(8,128)(2,1)} %copy-done.62) | copy-start | bytes 147460
  919.4 74.6 %reduce-scatter.52.cloned.1.call-start = ((), (), s32[]{:S(2)}) async-start(), calls=%async_computation.40 | async-start | bytes 442368 | tf_op jit(solution)/shard_map/reduce_scatter | solution.py:109
  965.5 120.5 %copy-start.42 = (f32[128,192]{0,1:T(8,128)}, f32[128,192]{0,1:T(8,128)S(1)}, u32[]{:S(2)}) copy-start(f32[128,192]{0,1:T(8,128)S(1)} %subtract_add_fusion.2) | copy-start | bytes 294916
  966.6 72.2 %reduce-scatter.60.cloned.1.call-start = ((), (), s32[]{:S(2)}) async-start(), calls=%async_computation.44 | async-start | bytes 294912
  1010.9 62.1 %copy-start.174 = (f32[128]{0:T(128)S(1)}, f32[128]{0:T(128)}, u32[]{:S(2)}) copy-start(f32[128]{0:T(128)} %get-tuple-element.125) | copy-start | bytes 1540
  1010.9 75.1 %copy-start.78 = (f32[128,192]{0,1:T(8,128)S(1)}, f32[128,192]{0,1:T(8,128)}, u32[]{:S(2)}) copy-start(f32[128,192]{0,1:T(8,128)} %get-tuple-element.45) | copy-start | bytes 294916
  1011.2 76.8 %copy-start.137 = (s32[1280]{0:T(1024)S(1)}, s32[1280]{0:T(1024)}, u32[]{:S(2)}) copy-start(s32[1280]{0:T(1024)} %get-tuple-element.100) | copy-start | bytes 15364
  1040.9 13.3 all-to-all-start.9
  1047.6 157.5 %reduce-scatter.54.cloned.1.call-start = ((), (), s32[]{:S(2)}) async-start(), calls=%async_computation.41 | async-start | bytes 442368 | tf_op jit(solution)/shard_map/reduce_scatter | solution.py:126
  1086.8 4.8 collective-permute-start.3
  1181.8 71.6 %reduce-scatter.56.cloned.1.call-start = ((), (), s32[]{:S(2)}) async-start(), calls=%async_computation.42 | async-start | bytes 442368 | tf_op jit(solution)/shard_map/reduce_scatter | solution.py:109
  1256.5 13.4 all-to-all-start.10
  1263.2 49.4 %reduce-scatter.62.cloned.1.call-start = ((), (), s32[]{:S(2)}) async-start(), calls=%async_computation.45 | async-start | bytes 294912
  1275.7 344.1 %reduce-scatter.44.cloned.1.call-start = ((), (), s32[]{:S(2)}) async-start(), calls=%async_computation.36 | async-start | bytes 442368 | tf_op jit(solution)/shard_map/reduce_scatter | solution.py:126
  1302.3 319.3 %reduce-scatter.66.cloned.1.call-start = ((), (), s32[]{:S(2)}) async-start(), calls=%async_computation.47 | async-start | bytes 884736
  1314.7 10.0 all-to-all-start.11
  1318.1 352.3 %reduce-scatter.64.cloned.1.call-start = ((), (), s32[]{:S(2)}) async-start(), calls=%async_computation.46 | async-start | bytes 1474560
  1350.1 322.1 %reduce-scatter.70.cloned.1.call-start = ((), (), s32[]{:S(2)}) async-start(), calls=%async_computation.49 | async-start | bytes 8847360
  1414.8 380.5 %reduce-scatter.68.cloned.1.call-start = ((), (), s32[]{:S(2)}) async-start(), calls=%async_computation.48 | async-start | bytes 17694720
  (159 other events, 2397.4 us)
Sparse Core Ops, SparseCore 0:
  24.4 30.8 reduce-scatter.33
  233.2 25.9 reduce-scatter.35
  281.9 28.1 reduce-scatter.37
  507.0 30.0 reduce-scatter.39
  541.5 29.8 reduce-scatter.45
  591.1 27.2 reduce-scatter.47
  621.4 30.3 reduce-scatter.41
  696.4 24.3 reduce-scatter.57
  919.5 28.1 reduce-scatter.49
  966.7 27.2 reduce-scatter.51
  1012.3 26.4 reduce-scatter.59
  1182.0 23.1 reduce-scatter.53
  1226.1 27.2 reduce-scatter.55
  1275.8 26.4 reduce-scatter.61
  1304.6 29.5 reduce-scatter.43
  1337.7 72.1 reduce-scatter.65
  1414.0 73.2 reduce-scatter.63
  1491.7 112.5 reduce-scatter.69
  1618.8 176.4 reduce-scatter.67
where the time goes:
time: 1840 us; the launch traced here: 1830 us
  blocking collectives  481 us (26%)
  local copies, waits for them, and re-layouts  466 us (25%)
  waiting for transfers between devices  397 us (22%)
  matrix products  277 us (15%)
  other arithmetic  119 us (6%)
  starting transfers between devices  67.7 us (4%)
    unnamed x408, local copies, waits for them, and re-layouts  220 us
    psum x14, blocking collectives, feature_total(): return lax.psum(values, 'wa')  208 us
    unnamed x26, waiting for transfers between devices  140 us
    reduce_scatter x6, waiting for transfers between devices, token_sum(): lax.psum_scatter(apply(left).astype(jnp.bfloat16), 'wa', scatter_dimensio...  104 us
    reduce_scatter x6, waiting for transfers between devices, feature_share(): lax.psum_scatter(values.astype(jnp.bfloat16), 'wa', scatter_dimension=1,...  102 us
    all_gather x6, blocking collectives, to_rows(): return lax.all_gather(values, 'wa', axis=0, tiled=True)  95.1 us
    all_gather x6, blocking collectives, features(): return lax.all_gather(values, 'wa', axis=1, tiled=True)  83.1 us
    dot_general x3, matrix products, on_device(): jnp.einsum('ech,ecd->ehd', gate_up_grad, expert_rows, preferred_element_t...  58.1 us
  transfers between devices with their start and end apart: 34, of which 22 were waited for; matrix products, arithmetic and copies ran while one was open for 27% of the time, Pallas kernels for 0%

commit v1 on v0

v1 whole, which is shorter than its diff:
```python
import jax
import jax.numpy as jnp
from jax import lax
from jax.experimental import pallas as pl
from jax.experimental.pallas import tpu as pltpu
from jax.sharding import PartitionSpec as P

HEADS = 24
KV_HEADS = 8
PER_GROUP = HEADS // KV_HEADS
HEAD_DIM = 64
EXPERTS = 40
TOP = 8
MICRO = 2
CAP = 32
N_SEQ = 8
N_WA = 8
ROWS = 128
WIDTH = 1536
OWN = WIDTH // N_WA
TOKENS = MICRO * ROWS
LENGTH = ROWS * N_SEQ
HIDDEN = 64
SLOTS = MICRO * CAP
GROUP_COLS = (PER_GROUP + 2) * HEAD_DIM
BATCH = 4
STEPS = EXPERTS // BATCH
BLOCK = BATCH * HIDDEN
SCALE = HEAD_DIM ** (-0.5)
EPSILON = 1e-06
BF16 = jnp.bfloat16
F32 = jnp.float32
VMEM_LIMIT = 56 * 1024 * 1024


def dot_nn(a, b):
    return lax.dot_general(a, b, (((1,), (0,)), ((), ())), preferred_element_type=F32)


def dot_nt(a, b):
    return lax.dot_general(a, b, (((1,), (1,)), ((), ())), preferred_element_type=F32)


def dot_tn(a, b):
    return lax.dot_general(a, b, (((0,), (0,)), ((), ())), preferred_element_type=F32)


def params():
    return pltpu.CompilerParams(
        vmem_limit_bytes=VMEM_LIMIT, dimension_semantics=("arbitrary",)
    )


def one_hot_slots(places):
    slot = lax.broadcasted_iota(jnp.int32, (BATCH, SLOTS, TOKENS), 1).astype(F32)
    hit = jnp.where(slot == places, 1.0, 0.0)
    return hit.reshape(BATCH * SLOTS, TOKENS).astype(BF16)


def own_slots(rows, pick, height):
    every = dot_nt(rows, pick)
    lane = lax.broadcasted_iota(jnp.int32, (height, BATCH * SLOTS), 1) // SLOTS
    out = every[:height]
    for e in range(1, BATCH):
        out = jnp.where(lane == e, every[e * height : (e + 1) * height], out)
    return out.astype(BF16)


def spread_slots(compact):
    lane = lax.broadcasted_iota(jnp.int32, compact.shape, 1) // SLOTS
    zero = jnp.zeros_like(compact)
    return jnp.concatenate([jnp.where(lane == e, compact, zero) for e in range(BATCH)], axis=0)


def experts_forward_kernel(
    x_ref, gate_ref, place_ref, win_ref, wout_ref, y_ref, g_ref, u_ref, f_ref, total
):
    step = pl.program_id(0)
    x = x_ref[...]
    wg = win_ref[:, 0].reshape(BLOCK, WIDTH)
    wu = win_ref[:, 1].reshape(BLOCK, WIDTH)
    g = dot_nn(wg, x)
    u = dot_nn(wu, x)
    g_ref[...] = g.astype(BF16)
    u_ref[...] = u.astype(BF16)
    active = (g * jax.nn.sigmoid(g) * u).astype(BF16).astype(F32)
    gated = (active.reshape(BATCH, HIDDEN, TOKENS) * gate_ref[...]).astype(BF16)
    gated = gated.reshape(BLOCK, TOKENS)
    f_ref[...] = own_slots(gated, one_hot_slots(place_ref[...]), HIDDEN)
    part = dot_tn(gated, wout_ref[...].reshape(BLOCK, WIDTH))

    @pl.when(step == 0)
    def _():
        total[...] = part

    @pl.when(step > 0)
    def _():
        total[...] += part

    @pl.when(step == STEPS - 1)
    def _():
        y_ref[...] = total[...].astype(BF16).T


def experts_forward(x, gates, places, w_in, w_out):
    return pl.pallas_call(
        experts_forward_kernel,
        grid=(STEPS,),
        in_specs=[
            pl.BlockSpec((WIDTH, TOKENS), lambda i: (0, 0)),
            pl.BlockSpec((BATCH, 1, TOKENS), lambda i: (i, 0, 0)),
            pl.BlockSpec((BATCH, 1, TOKENS), lambda i: (i, 0, 0)),
            pl.BlockSpec((BATCH, 2, HIDDEN, WIDTH), lambda i: (i, 0, 0, 0)),
            pl.BlockSpec((BATCH, HIDDEN, WIDTH), lambda i: (i, 0, 0)),
        ],
        out_specs=[
            pl.BlockSpec((WIDTH, TOKENS), lambda i: (0, 0)),
            pl.BlockSpec((BLOCK, TOKENS), lambda i: (i, 0)),
            pl.BlockSpec((BLOCK, TOKENS), lambda i: (i, 0)),
            pl.BlockSpec((HIDDEN, BATCH * SLOTS), lambda i: (0, i)),
        ],
        out_shape=[
            jax.ShapeDtypeStruct((WIDTH, TOKENS), BF16),
            jax.ShapeDtypeStruct((EXPERTS * HIDDEN, TOKENS), BF16),
            jax.ShapeDtypeStruct((EXPERTS * HIDDEN, TOKENS), BF16),
            jax.ShapeDtypeStruct((HIDDEN, EXPERTS * SLOTS), BF16),
        ],
        scratch_shapes=[pltpu.VMEM((TOKENS, WIDTH), F32)],
        compiler_params=params(),
        cost_estimate=pl.CostEstimate(
            flops=6 * TOKENS * EXPERTS * HIDDEN * WIDTH, bytes_accessed=28_000_000, transcendentals=0
        ),
        name="experts_forward",
    )(x, gates, places, w_in, w_out)


def experts_backward_kernel(
    dz_ref, g_ref, u_ref, gate_ref, place_ref, win_ref, wout_ref, dx_ref, dgate_ref, du_ref, total
):
    step = pl.program_id(0)
    through = dot_nn(wout_ref[...].reshape(BLOCK, WIDTH), dz_ref[...])
    g = g_ref[...].astype(F32)
    u = u_ref[...].astype(F32)
    sig = jax.nn.sigmoid(g)
    silu = g * sig
    active = (silu * u).astype(BF16).astype(F32)
    dgate_ref[...] = jnp.sum(
        (active * through).reshape(BATCH, HIDDEN, TOKENS), axis=1, keepdims=True
    )
    df = (through.reshape(BATCH, HIDDEN, TOKENS) * gate_ref[...]).reshape(BLOCK, TOKENS)
    dg = (df * u * (sig * (1.0 + g * (1.0 - sig)))).astype(BF16)
    du = (df * silu).astype(BF16)
    pick = one_hot_slots(place_ref[...])
    du_ref[:HIDDEN] = own_slots(dg, pick, HIDDEN)
    du_ref[HIDDEN:] = own_slots(du, pick, HIDDEN)
    part = dot_tn(dg, win_ref[:, 0].reshape(BLOCK, WIDTH))
    part += dot_tn(du, win_ref[:, 1].reshape(BLOCK, WIDTH))

    @pl.when(step == 0)
    def _():
        total[...] = part

    @pl.when(step > 0)
    def _():
        total[...] += part

    @pl.when(step == STEPS - 1)
    def _():
        dx_ref[...] = total[...].astype(BF16).T


def experts_backward(dz, g, u, gates, places, w_in, w_out):
    return pl.pallas_call(
        experts_backward_kernel,
        grid=(STEPS,),
        in_specs=[
            pl.BlockSpec((WIDTH, TOKENS), lambda i: (0, 0)),
            pl.BlockSpec((BLOCK, TOKENS), lambda i: (i, 0)),
            pl.BlockSpec((BLOCK, TOKENS), lambda i: (i, 0)),
            pl.BlockSpec((BATCH, 1, TOKENS), lambda i: (i, 0, 0)),
            pl.BlockSpec((BATCH, 1, TOKENS), lambda i: (i, 0, 0)),
            pl.BlockSpec((BATCH, 2, HIDDEN, WIDTH), lambda i: (i, 0, 0, 0)),
            pl.BlockSpec((BATCH, HIDDEN, WIDTH), lambda i: (i, 0, 0)),
        ],
        out_specs=[
            pl.BlockSpec((WIDTH, TOKENS), lambda i: (0, 0)),
            pl.BlockSpec((BATCH, 1, TOKENS), lambda i: (i, 0, 0)),
            pl.BlockSpec((2 * HIDDEN, BATCH * SLOTS), lambda i: (0, i)),
        ],
        out_shape=[
            jax.ShapeDtypeStruct((WIDTH, TOKENS), BF16),
            jax.ShapeDtypeStruct((EXPERTS, 1, TOKENS), F32),
            jax.ShapeDtypeStruct((2 * HIDDEN, EXPERTS * SLOTS), BF16),
        ],
        scratch_shapes=[pltpu.VMEM((TOKENS, WIDTH), F32)],
        compiler_params=params(),
        cost_estimate=pl.CostEstimate(
            flops=6 * TOKENS * EXPERTS * HIDDEN * WIDTH, bytes_accessed=28_000_000, transcendentals=0
        ),
        name="experts_backward",
    )(dz, g, u, gates, places, w_in, w_out)


def weight_grad_kernel(compact_ref, feature_ref, place_ref, out_ref):
    height = compact_ref.shape[1]
    total = jnp.zeros((BATCH * height, OWN), F32)
    for s in range(N_SEQ):
        pick = one_hot_slots(place_ref[s])
        rows = dot_nt(feature_ref[s], pick).astype(BF16)
        total += dot_nt(spread_slots(compact_ref[s]), rows)
    out_ref[...] = total.reshape(BATCH, height, OWN)


def weight_grad(compact, feature, places):
    height = compact.shape[1]
    return pl.pallas_call(
        weight_grad_kernel,
        grid=(STEPS,),
        in_specs=[
            pl.BlockSpec((N_SEQ, height, BATCH * SLOTS), lambda i: (0, 0, i)),
            pl.BlockSpec((N_SEQ, OWN, TOKENS), lambda i: (0, 0, 0)),
            pl.BlockSpec((N_SEQ, BATCH, 1, TOKENS), lambda i: (0, i, 0, 0)),
        ],
        out_specs=pl.BlockSpec((BATCH, height, OWN), lambda i: (i, 0, 0)),
        out_shape=jax.ShapeDtypeStruct((EXPERTS, height, OWN), F32),
        compiler_params=params(),
        cost_estimate=pl.CostEstimate(
            flops=4 * N_SEQ * TOKENS * EXPERTS * height * OWN, bytes_accessed=15_000_000, transcendentals=0
        ),
        name="expert_weight_grad",
    )(compact, feature, places)


def causal_mask(first):
    key = lax.broadcasted_iota(jnp.int32, (LENGTH, ROWS), 0)
    query = lax.broadcasted_iota(jnp.int32, (LENGTH, ROWS), 1) + first
    return key <= query


def side_by_side(parts):
    return jnp.concatenate(parts, axis=1)


def attention_forward_kernel(first_ref, q_ref, kv_ref, o_ref, lse_ref):
    keys = side_by_side([kv_ref[s, :HEAD_DIM] for s in range(N_SEQ)])
    values = side_by_side([kv_ref[s, HEAD_DIM:] for s in range(N_SEQ)])
    keep = causal_mask(first_ref[0])
    for h in range(PER_GROUP):
        rows = slice(h * HEAD_DIM, (h + 1) * HEAD_DIM)
        scores = jnp.where(keep, dot_tn(keys, q_ref[rows]) * SCALE, -1e30)
        top = jnp.max(scores, axis=0, keepdims=True)
        raised = jnp.exp(scores - top)
        total = jnp.sum(raised, axis=0, keepdims=True)
        probs = (raised * (1.0 / total)).astype(BF16)
        o_ref[rows] = dot_nn(values, probs).astype(BF16)
        lse_ref[h] = top + jnp.log(total)


def attention_forward(first, q, kv):
    return pl.pallas_call(
        attention_forward_kernel,
        grid=(MICRO,),
        in_specs=[
            pl.BlockSpec(memory_space=pltpu.SMEM),
            pl.BlockSpec((PER_GROUP * HEAD_DIM, ROWS), lambda m: (0, m)),
            pl.BlockSpec((N_SEQ, 2 * HEAD_DIM, ROWS), lambda m: (0, 0, m)),
        ],
        out_specs=[
            pl.BlockSpec((PER_GROUP * HEAD_DIM, ROWS), lambda m: (0, m)),
            pl.BlockSpec((PER_GROUP, 1, ROWS), lambda m: (0, 0, m)),
        ],
        out_shape=[
            jax.ShapeDtypeStruct((PER_GROUP * HEAD_DIM, TOKENS), BF16),
            jax.ShapeDtypeStruct((PER_GROUP, 1, TOKENS), F32),
        ],
        compiler_params=params(),
        name="attention_forward",
    )(first, q, kv)


def attention_backward_kernel(first_ref, q_ref, kv_ref, o_ref, do_ref, lse_ref, dq_ref, dkv_ref):
    keys = side_by_side([kv_ref[s, :HEAD_DIM] for s in range(N_SEQ)])
    values = side_by_side([kv_ref[s, HEAD_DIM:] for s in range(N_SEQ)])
    keep = causal_mask(first_ref[0])
    dkeys = jnp.zeros((HEAD_DIM, LENGTH), F32)
    dvalues = jnp.zeros((HEAD_DIM, LENGTH), F32)
    for h in range(PER_GROUP):
        rows = slice(h * HEAD_DIM, (h + 1) * HEAD_DIM)
        query = q_ref[rows]
        dout = do_ref[rows]
        scores = jnp.where(keep, dot_tn(keys, query) * SCALE, -1e30)
        probs = jnp.exp(scores - lse_ref[h])
        dvalues += dot_nt(dout, probs.astype(BF16))
        inner = jnp.sum(
            dout.astype(F32) * o_ref[rows].astype(F32), axis=0, keepdims=True
        )
        dscores = (probs * (dot_tn(values, dout) - inner)).astype(BF16)
        dkeys += dot_nt(query, dscores)
        dq_ref[rows] = dot_nn(keys, dscores) * SCALE
    dkeys = (dkeys * SCALE).astype(BF16)
    dvalues = dvalues.astype(BF16)
    for s in range(N_SEQ):
        lanes = slice(s * ROWS, (s + 1) * ROWS)
        dkv_ref[s, :HEAD_DIM] = dkeys[:, lanes]
        dkv_ref[s, HEAD_DIM:] = dvalues[:, lanes]


def attention_backward(first, q, kv, o, do, lse):
    q_spec = pl.BlockSpec((PER_GROUP * HEAD_DIM, ROWS), lambda m: (0, m))
    kv_spec = pl.BlockSpec((N_SEQ, 2 * HEAD_DIM, ROWS), lambda m: (0, 0, m))
    return pl.pallas_call(
        attention_backward_kernel,
        grid=(MICRO,),
        in_specs=[
            pl.BlockSpec(memory_space=pltpu.SMEM),
            q_spec,
            kv_spec,
            q_spec,
            q_spec,
            pl.BlockSpec((PER_GROUP, 1, ROWS), lambda m: (0, 0, m)),
        ],
        out_specs=[q_spec, kv_spec],
        out_shape=[
            jax.ShapeDtypeStruct((PER_GROUP * HEAD_DIM, TOKENS), F32),
            jax.ShapeDtypeStruct((N_SEQ, 2 * HEAD_DIM, TOKENS), BF16),
        ],
        compiler_params=params(),
        name="attention_backward",
    )(first, q, kv, o, do, lse)


def rotate(values, cosine, sine):
    half = HEAD_DIM // 2
    a, b = values[:, :half], values[:, half:]
    return jnp.concatenate([a * cosine - b * sine, b * cosine + a * sine], axis=1)


def high_low(values):
    high = values.astype(BF16)
    return high, (values - high.astype(F32)).astype(BF16)


def exchange(blocks, axis):
    return lax.all_to_all(blocks, axis, split_axis=0, concat_axis=0, tiled=False)


def summed(blocks, axis):
    return jnp.sum(exchange(blocks, axis).astype(F32), axis=0)


def on_device(
    first_layer_input,
    routes,
    cotangent,
    gains,
    qkv_weight,
    out_weight,
    router_weight,
    expert_in,
    expert_out,
):
    section_first = lax.axis_index("section") == 0
    s_index = lax.axis_index("seq")
    w_index = lax.axis_index("wa")
    first = jnp.reshape(s_index * ROWS, (1,)).astype(jnp.int32)

    def rows_of(values):
        return lax.all_gather(values, "wa", axis=0, tiled=True)

    def own(values):
        return lax.dynamic_slice_in_dim(values, w_index * OWN, OWN, 0)

    def lanes(values):
        return jnp.concatenate([values[0], values[1]], axis=1)

    def of_section(one, two):
        return jnp.where(section_first, one, two)

    x_first = lanes(first_layer_input)
    cot = lanes(cotangent)
    x_first_full = rows_of(x_first)
    w_qkv = qkv_weight[0]
    w_qkv_group = exchange(
        jnp.transpose(w_qkv.reshape(OWN, KV_HEADS, GROUP_COLS), (1, 0, 2)), "wa"
    ).reshape(WIDTH, GROUP_COLS)
    small = rows_of(jnp.concatenate([gains[0].T, router_weight[0].astype(F32)], axis=1))
    gain_one, gain_two = small[:, 0:1], small[:, 1:2]
    w_router = small[:, 2:].astype(BF16)
    w_attn_full = rows_of(out_weight[0])
    w_attn_group = lax.dynamic_slice_in_dim(w_attn_full, w_index * OWN, OWN, 1)
    cot_full = rows_of(cot)
    w_in = expert_in[0]
    w_out = expert_out[0]
    own_gain_one = gains[0, 0][:, None]
    own_gain_two = gains[0, 1][:, None]

    position = (s_index * ROWS + jnp.arange(ROWS, dtype=jnp.int32)).astype(F32)
    frequency = 10000.0 ** (
        -jnp.arange(HEAD_DIM // 2).astype(F32) * (2.0 / HEAD_DIM)
    )
    angle = frequency[:, None] * position[None, :]
    cosine = jnp.tile(jnp.cos(angle), (1, MICRO))
    sine = jnp.tile(jnp.sin(angle), (1, MICRO))

    experts = jnp.arange(EXPERTS, dtype=jnp.int32)[None, :, None]
    chosen = jnp.zeros((MICRO, EXPERTS, ROWS), F32)
    for k in range(TOP):
        chosen += (routes[0][:, None, :, k] == experts).astype(F32)
    earlier = jnp.triu(jnp.ones((ROWS, ROWS), BF16), 1)
    rank = jnp.einsum("met,tu->meu", chosen.astype(BF16), earlier, preferred_element_type=F32)
    micro = jnp.arange(MICRO, dtype=jnp.int32).astype(F32)[:, None, None]
    place = lanes(jnp.where(chosen > 0.5, rank + CAP * micro, -1.0))
    chosen = lanes(chosen) > 0.5
    places_all = lax.all_gather(place.astype(BF16), "seq", axis=0, tiled=False)
    places_all = places_all.astype(F32)[:, :, None, :]
    places = place[:, None, :]
    route_lanes = jnp.concatenate([routes[0, 0].T, routes[0, 1].T], axis=1)
    picked = (
        route_lanes[:, None, :] == jnp.arange(EXPERTS, dtype=jnp.int32)[None, :, None]
    )

    def norm_scale(values):
        return lax.rsqrt(jnp.mean(values * values, axis=0, keepdims=True) + EPSILON)

    def forward(x_own, x_full):
        x = x_full.astype(F32)
        scale_one = norm_scale(x)
        normed_one = (x * scale_one * gain_one).astype(BF16)
        heads = dot_tn(w_qkv_group, normed_one).reshape(PER_GROUP + 2, HEAD_DIM, TOKENS)
        turned = rotate(heads[: PER_GROUP + 1], cosine, sine)
        turned = jnp.concatenate([turned, heads[PER_GROUP + 1 :]], axis=0).astype(BF16)
        turned = turned.reshape(GROUP_COLS, TOKENS)
        queries = turned[: PER_GROUP * HEAD_DIM]
        key_value = exchange(
            jnp.broadcast_to(
                turned[PER_GROUP * HEAD_DIM :][None], (N_SEQ, 2 * HEAD_DIM, TOKENS)
            ),
            "seq",
        )
        mixed, log_total = attention_forward(first, queries, key_value)
        mixed_full = rows_of(mixed)
        middle = x + dot_nn(w_attn_full, mixed_full)
        scale_two = norm_scale(middle)
        normed_two = (middle * scale_two * gain_two).astype(BF16)
        logits = dot_tn(w_router, normed_two)
        raised = jnp.where(
            chosen,
            jnp.exp(logits - jnp.max(jnp.where(chosen, logits, -1e30), axis=0, keepdims=True)),
            0.0,
        )
        gates = raised / jnp.sum(raised, axis=0, keepdims=True)
        part, g, u, compact = experts_forward(
            normed_two, gates[:, None, :], places, w_in, w_out
        )
        out = own(middle) + summed(part.reshape(N_WA, OWN, TOKENS), "wa")
        saved = (
            x_own,
            scale_one,
            own(normed_one),
            queries,
            key_value,
            log_total,
            mixed,
            mixed_full,
            middle,
            scale_two,
            normed_two,
            logits,
            gates,
            g,
            u,
        )
        return out.astype(BF16), compact, saved

    def backward(dz, dz_full, saved):
        (
            x_own,
            scale_one,
            own_normed_one,
            queries,
            key_value,
            log_total,
            mixed,
            mixed_full,
            middle,
            scale_two,
            normed_two,
            logits,
            gates,
            g,
            u,
        ) = saved
        part, dgate, du = experts_backward(
            dz_full, g, u, gates[:, None, :], places, w_in, w_out
        )
        inner = jnp.sum(part.astype(F32) * middle * gain_two, axis=0, keepdims=True)
        dgate_top = jnp.sum(jnp.where(picked, dgate[:, 0][None], 0.0), axis=1)
        extra = jnp.concatenate(
            [
                dgate_top.astype(BF16),
                *high_low(inner),
                jnp.zeros((16 - TOP - 2, TOKENS), BF16),
            ],
            axis=0,
        )
        blocks = jnp.concatenate(
            [
                part.reshape(N_WA, OWN, TOKENS),
                jnp.broadcast_to(extra[None], (N_WA, 16, TOKENS)),
            ],
            axis=1,
        )
        back = summed(blocks, "wa")
        dgate_top = back[OWN : OWN + TOP]
        inner = back[OWN + TOP : OWN + TOP + 1] + back[OWN + TOP + 1 : OWN + TOP + 2]
        dgate = jnp.sum(jnp.where(picked, dgate_top[:, None, :], 0.0), axis=0)
        dlogit = gates * (dgate - jnp.sum(gates * dgate, axis=0, keepdims=True))
        dlogit_high, dlogit_low = high_low(dlogit)
        own_router = router_weight[0]
        dnormed = back[:OWN] + dot_nn(own_router, dlogit_high) + dot_nn(own_router, dlogit_low)
        inner += jnp.sum(dlogit * logits, axis=0, keepdims=True) / scale_two
        own_middle = own(middle)
        dmiddle = (
            dz.astype(F32)
            + scale_two * own_gain_two * dnormed
            - own_middle * (scale_two * scale_two * scale_two * inner * (1.0 / WIDTH))
        )
        gain_two_grad = jnp.sum(dnormed * own_middle * scale_two, axis=1, keepdims=True)
        own_normed_two = own(normed_two)
        router_grad = dot_nt(own_normed_two, dlogit_high) + dot_nt(own_normed_two, dlogit_low)
        dmiddle_low = dmiddle.astype(BF16)
        attn_grad = dot_nt(dmiddle_low, mixed_full)
        dmixed = dot_tn(w_attn_group, rows_of(dmiddle_low)).astype(BF16)
        dq, dkv = attention_backward(first, queries, key_value, mixed, dmixed, log_total)
        dkv = summed(dkv, "seq")
        dturned = jnp.concatenate([dq, dkv], axis=0)
        turned = jnp.concatenate(
            [queries, lax.dynamic_index_in_dim(key_value, s_index, 0, False)], axis=0
        )
        inner_one = jnp.sum(dturned * turned.astype(F32), axis=0, keepdims=True)
        dheads = dturned.reshape(PER_GROUP + 2, HEAD_DIM, TOKENS)
        dheads = jnp.concatenate(
            [rotate(dheads[: PER_GROUP + 1], cosine, -sine), dheads[PER_GROUP + 1 :]], axis=0
        )
        full = lax.all_gather(
            jnp.concatenate(
                [
                    dheads.reshape(GROUP_COLS, TOKENS).astype(BF16),
                    *high_low(inner_one),
                    jnp.zeros((14, TOKENS), BF16),
                ],
                axis=0,
            ),
            "wa",
            axis=0,
            tiled=False,
        )
        dheads_full = full[:, :GROUP_COLS].reshape(KV_HEADS * GROUP_COLS, TOKENS)
        inner_one = jnp.sum(
            full[:, GROUP_COLS : GROUP_COLS + 2].astype(F32), axis=(0, 1)
        )[None] / scale_one
        dnormed_one = dot_nn(w_qkv, dheads_full)
        x = x_own.astype(F32)
        dx = (
            dmiddle
            + scale_one * own_gain_one * dnormed_one
            - x * (scale_one * scale_one * scale_one * inner_one * (1.0 / WIDTH))
        )
        gain_one_grad = jnp.sum(dnormed_one * x * scale_one, axis=1, keepdims=True)
        qkv_grad = dot_nt(own_normed_one, dheads_full)
        return dx, du, gain_one_grad, gain_two_grad, router_grad, attn_grad, qkv_grad

    out_one, compact_one, saved_one = forward(x_first, x_first_full)
    received = lax.ppermute(out_one, "section", [(0, 1)])
    out_two, compact_two, saved_two = forward(received, rows_of(received))

    feature_in = exchange(
        of_section(saved_one[10], saved_two[10]).reshape(N_SEQ, OWN, TOKENS), "seq"
    )
    compact_out = lax.all_gather(of_section(compact_one, compact_two), "seq", axis=0, tiled=False)

    back_two = backward(cot, cot_full, saved_two)
    returned = lax.ppermute(back_two[0].astype(BF16), "section", [(1, 0)])
    returned_full = rows_of(returned)
    feature_out = exchange(
        of_section(returned_full, cot_full).reshape(N_SEQ, OWN, TOKENS), "seq"
    )
    expert_out_grad = weight_grad(compact_out, feature_out, places_all)
    back_one = backward(returned, returned_full, saved_one)

    compact_in = lax.all_gather(of_section(back_one[1], back_two[1]), "seq", axis=0, tiled=False)
    expert_in_grad = weight_grad(compact_in, feature_in, places_all)
    gain_one_grad, gain_two_grad, router_grad, attn_grad, qkv_grad = (
        of_section(one, two) for one, two in zip(back_one[2:], back_two[2:])
    )
    small_grad = lax.psum(jnp.concatenate([gain_two_grad, router_grad], axis=1), "seq")
    attn_grad = summed(
        jnp.transpose(attn_grad.astype(BF16).reshape(OWN, N_SEQ, OWN), (1, 0, 2)), "seq"
    )
    qkv_blocks = jnp.transpose(
        qkv_grad.astype(BF16).reshape(OWN, N_SEQ, GROUP_COLS), (1, 0, 2)
    )
    gain_blocks = jnp.concatenate(
        [*high_low(gain_one_grad), jnp.zeros((OWN, 384 - GROUP_COLS - 2), BF16)], axis=1
    )
    qkv_grad = summed(
        jnp.concatenate(
            [qkv_blocks, jnp.broadcast_to(gain_blocks[None], (N_SEQ,) + gain_blocks.shape)],
            axis=2,
        ),
        "seq",
    )
    gain_one_grad = qkv_grad[:, GROUP_COLS] + qkv_grad[:, GROUP_COLS + 1]

    def tokens_first(values):
        return jnp.transpose(values.reshape(OWN, MICRO, ROWS), (1, 2, 0))[None]

    return (
        tokens_first(of_section(out_one, out_two)),
        tokens_first(of_section(back_one[0], back_two[0])),
        jnp.stack([gain_one_grad, small_grad[:, 0]])[None],
        qkv_grad[None, :, :GROUP_COLS],
        attn_grad[None],
        small_grad[None, :, 1:],
        expert_in_grad.reshape(1, EXPERTS, 2, HIDDEN, OWN),
        expert_out_grad[None],
    )


def solution(mesh):
    return jax.shard_map(
        on_device,
        mesh=mesh,
        in_specs=(
            P(None, "wa", "seq"),
            P("section", None, "seq", None),
            P(None, "wa", "seq"),
            P("section", None, "wa"),
            P("section", "wa", None),
            P("section", "wa", None),
            P("section", "wa", None),
            P("section", None, None, "wa", None),
            P("section", None, "wa", None),
        ),
        out_specs=(
            P("section", None, "seq", "wa"),
            P("section", None, "seq", "wa"),
            P("section", None, "wa"),
            P("section", "wa", "seq"),
            P("section", "wa", "seq"),
            P("section", "wa", None),
            P("section", None, None, "wa", "seq"),
            P("section", None, "wa", "seq"),
        ),
        check_vma=False,
    )
```

time: 1840 us -> 670 us (0.36)
  local copies, waits for them, and re-layouts: 466 us -> 31.7 us
  waiting for transfers between devices: 397 us -> 123 us
  blocking collectives: 481 us -> 227 us
  matrix products: 277 us -> 33.9 us
  Pallas kernels: 0 us -> 127 us
  other arithmetic: 119 us -> 29 us
    dot_general x69 -> x23, matrix products: 277 us -> 33.9 us  [the longest x8 14.2 us: dot_nn(): lax.dot_general(a, b, (((1,), (0,)), ((), ())), preferred_element_type=F32)]
    unnamed x408 -> x235, local copies, waits for them, and re-layouts: 220 us -> 6.09 us
    psum x15 -> x1, blocking collectives: 242 us -> 35.5 us  [on_device(): lax.psum(jnp.concatenate([gain_two_grad, router_grad], axis=1), 'seq')]
    reduce_scatter x12 -> x0, waiting for transfers between devices: 205 us -> none  [the longest x6 104 us: token_sum(): lax.psum_scatter(apply(left).astype(jnp.bfloat16), 'wa', scatter_dimensio...]
    gather x33 -> x0, local copies, waits for them, and re-layouts: 158 us -> none  [the longest x3 33.2 us: on_device(): token_grad = jnp.sum(row_grad[slots].reshape(rows, TOP, width), axis=1)]
    unnamed x26 -> x5, waiting for transfers between devices: 140 us -> 0.75 us
    pallas_call x0 -> x10, Pallas kernels: none -> 127 us  [the longest x2 40 us: experts_backward(): pl.pallas_call(experts_backward_kernel, grid=(STEPS,), in_specs=[pl.Block...]
    all_gather x15 -> x10, blocking collectives: 227 us -> 176 us  [the longest x9 148 us: rows_of(): return lax.all_gather(values, 'wa', axis=0, tiled=True)]
  transfers between devices with their start and end apart: 34 -> 19, of which waited for: 22 -> 11; matrix products, arithmetic and copies ran while one was open for 27% -> 8% of each run, Pallas kernels for 0% -> 3%
where the time goes in v1:
time: 670 us; the launch traced here: 658 us
  blocking collectives  227 us (34%)
  Pallas kernels  127 us (19%)
  waiting for transfers between devices  123 us (18%)
  starting transfers between devices  70.2 us (10%)
  matrix products  33.9 us (5%)
  local copies, waits for them, and re-layouts  31.7 us (5%)
  other arithmetic  29 us (4%)
  between operations  16.1 us (2%)
    all_gather x9, blocking collectives, rows_of(): return lax.all_gather(values, 'wa', axis=0, tiled=True)  148 us
    all_to_all x12, waiting for transfers between devices, exchange(): lax.all_to_all(blocks, axis, split_axis=0, concat_axis=0, tiled=False)  67.6 us
    all_to_all x12, starting transfers between devices, exchange(): lax.all_to_all(blocks, axis, split_axis=0, concat_axis=0, tiled=False)  65.5 us
    pallas_call x2, Pallas kernels, experts_backward(): pl.pallas_call(experts_backward_kernel, grid=(STEPS,), in_specs=[pl.Block...  40 us
    psum x1, blocking collectives, on_device(): lax.psum(jnp.concatenate([gain_two_grad, router_grad], axis=1), 'seq')  35.5 us
    pallas_call x2, Pallas kernels, experts_forward(): pl.pallas_call(experts_forward_kernel, grid=(STEPS,), in_specs=[pl.BlockS...  34.9 us
    pallas_call x2, Pallas kernels, weight_grad(): pl.pallas_call(weight_grad_kernel, grid=(STEPS,), in_specs=[pl.BlockSpec(...  32.1 us
    all_gather x1, blocking collectives, on_device(): places_all = lax.all_gather(place.astype(BF16), 'seq', axis=0, tiled=False)  28.3 us
  transfers between devices with their start and end apart: 19, of which 11 were waited for; matrix products, arithmetic and copies ran while one was open for 8% of the time, Pallas kernels for 3%

profile of v1, /device:TPU:1, one launch (start us, length us, event | category | flops | bytes accessed | tf_op | source)
XLA Modules:
  0.0 657.9 jit_solution(3537559659920081657)
XLA Ops:
  7.9 2.0 reshape_squeeze.3
  11.1 5.9 all-to-all-start
  18.5 31.4 %all_gather.58 = bf16[1536,256]{1,0:T(8,128)(2,1)S(1)} all-gather(bf16[192,256]{1,0:T(8,128)(2,1)S(1)} %pad_maximum_fusion.9), channel_id=1, replica_groups=mesh['section'=2,'seq'=8,'wa'=8] {'wa'}, dimensions={0}, use_global_device_ids=true | all-gather | bytes 884736 | tf_op jit(solution)/shard_map/all_gather | solution.py:368
  50.4 13.5 %all-gather.5 = f32[8,192,42]{1,2,0:T(8,128)S(1)} all-gather(f32[1,192,42]{1,2,0:T(8,128)S(1)} %maximum_bitcast_fusion), channel_id=1, replica_groups=mesh['section'=2,'seq'=8,'wa'=8] {'wa'}, dimensions={0}, use_global_device_ids=true | all-gather | bytes 290304 | tf_op jit(solution)/shard_map/all_gather | solution.py:368
  67.1 7.9 %all-to-all-start.1 = ((bf16[8,128,256]{2,1,0:T(8,128)(2,1)}), bf16[8,128,256]{2,1,0:T(8,128)(2,1)S(1)}, u32[]{:S(2)}, u32[]{:S(2)}) async-start(bf16[8,128,256]{2,1,0:T(8,128)(2,1)} %broadcast_in_dim.167), calls=%async_computation.1 | async-start | bytes 1048576 | tf_op jit(solution)/shard_map/all_to_all | solution.py:344
  77.1 8.5 %all-to-all-done.1.kv_ref = bf16[8,128,256]{2,1,0:T(8,128)(2,1)S(1)} async-done(((bf16[8,128,256]{2,1,0:T(8,128)(2,1)}), bf16[8,128,256]{2,1,0:T(8,128)(2,1)S(1)}, u32[]{:S(2)}, u32[]{:S(2)}) %all-to-all-start.1) | async-done | bytes 524320 | tf_op jit(solution)/shard_map/all_to_all | solution.py:344
  86.4 5.1 attention_forward.2
  91.5 15.6 %all_gather.60 = bf16[1536,256]{1,0:T(8,128)(2,1)} all-gather(bf16[192,256]{1,0:T(8,128)(2,1)} %get-tuple-element.30.o_ref), channel_id=1, replica_groups=mesh['section'=2,'seq'=8,'wa'=8] {'wa'}, dimensions={0}, use_global_device_ids=true | all-gather | bytes 884736 | tf_op jit(solution)/shard_map/all_gather | solution.py:368
  107.2 4.0 multiply_reduce_fusion.3
  113.1 17.4 %experts_forward.2 = (bf16[1536,256]{1,0:T(8,128)(2,1)}, bf16[2560,256]{1,0:T(8,128)(2,1)}, bf16[2560,256]{1,0:T(8,128)(2,1)}, bf16[64,2560]{1,0:T(8,128)(2,1)}) custom-call(bf16[1536,256]{1,0:T(8,128)(2,1)} %copy-done.2, f32[40,1,256]{2,1,0:T(1,128)} %copy.62.gate_ref, f32[40,1,256]{2,1,0:T(1,128)} %broadcast_in_dim.174.place_ref, ...), custom_call_target="tpu_custom_call" | custom-call | flops 6039797760 | bytes 28000000 | tf_op jit(solution)/shard_map/experts_forward/pallas_call | solution.py:106
  130.6 4.0 all-to-all-start.2
  137.3 9.5 %all-to-all-done.2 = bf16[8,192,256]{2,1,0:T(8,128)(2,1)S(1)} async-done(((bf16[8,192,256]{2,1,0:T(8,128)(2,1)}), bf16[8,192,256]{2,1,0:T(8,128)(2,1)S(1)}, u32[]{:S(2)}, u32[]{:S(2)}) %all-to-all-start.2) | async-done | bytes 786464 | tf_op jit(solution)/shard_map/all_to_all | solution.py:344
  147.0 3.0 collective-permute-start
  151.6 15.0 %all_gather.62 = bf16[1536,256]{1,0:T(8,128)(2,1)S(1)} all-gather(bf16[192,256]{1,0:T(8,128)(2,1)S(1)} %collective-permute-done), channel_id=1, replica_groups=mesh['section'=2,'seq'=8,'wa'=8] {'wa'}, dimensions={0}, use_global_device_ids=true | all-gather | bytes 884736 | tf_op jit(solution)/shard_map/all_gather | solution.py:368
  169.0 3.9 all-to-all-start.3
  173.0 14.9 %all_gather.64.dz_ref = bf16[1536,256]{1,0:T(8,128)(2,1)} all-gather(bf16[192,256]{1,0:T(8,128)(2,1)S(1)} %copy-done.51), channel_id=1, replica_groups=mesh['section'=2,'seq'=8,'wa'=8] {'wa'}, dimensions={0}, use_global_device_ids=true | all-gather | bytes 884736 | tf_op jit(solution)/shard_map/all_gather | solution.py:368
  189.3 5.1 attention_forward.3
  194.4 13.7 %all_gather.63 = bf16[1536,256]{1,0:T(8,128)(2,1)S(1)} all-gather(bf16[192,256]{1,0:T(8,128)(2,1)} %get-tuple-element.32.o_ref), channel_id=1, replica_groups=mesh['section'=2,'seq'=8,'wa'=8] {'wa'}, dimensions={0}, use_global_device_ids=true | all-gather | bytes 884736 | tf_op jit(solution)/shard_map/all_gather | solution.py:368
  208.1 4.3 multiply_reduce_fusion.2
  214.8 17.5 %experts_forward.3 = (bf16[1536,256]{1,0:T(8,128)(2,1)}, bf16[2560,256]{1,0:T(8,128)(2,1)}, bf16[2560,256]{1,0:T(8,128)(2,1)}, bf16[64,2560]{1,0:T(8,128)(2,1)}) custom-call(bf16[1536,256]{1,0:T(8,128)(2,1)} %copy-done.1, f32[40,1,256]{2,1,0:T(1,128)} %copy.64.gate_ref, f32[40,1,256]{2,1,0:T(1,128)} %broadcast_in_dim.174.place_ref, ...), custom_call_target="tpu_custom_call" | custom-call | flops 6039797760 | bytes 28000000 | tf_op jit(solution)/shard_map/experts_forward/pallas_call | solution.py:106
  232.3 20.0 %experts_backward.2 = (bf16[1536,256]{1,0:T(8,128)(2,1)}, f32[40,1,256]{2,1,0:T(1,128)}, bf16[128,2560]{1,0:T(8,128)(2,1)}) custom-call(bf16[1536,256]{1,0:T(8,128)(2,1)} %all_gather.64.dz_ref, bf16[2560,256]{1,0:T(8,128)(2,1)} %get-tuple-element.34.g_ref, bf16[2560,256]{1,0:T(8,128)(2,1)} %get-tuple-element.35.u_ref, f32[40,1,256]{2,1,0:T(1,128)} %copy.64.gate_ref, ...), custom_call_target="tpu_custom_call" | custom-call | flops 6039797760 | bytes 28000000 | tf_op jit(solution)/shard_map/experts_backward/pallas_call | solution.py:173
  252.3 1.5 multiply_reduce_fusion.1
  255.0 4.4 all-to-all-start.5
  260.0 12.5 %all-to-all-done.5 = bf16[8,208,256]{2,1,0:T(8,128)(2,1)} async-done(((bf16[8,208,256]{2,1,0:T(8,128)(2,1)}), bf16[8,208,256]{2,1,0:T(8,128)(2,1)}, u32[]{:S(2)}, u32[]{:S(2)}) %all-to-all-start.5) | async-done | bytes 852000 | tf_op jit(solution)/shard_map/all_to_all | solution.py:344
  274.3 1.7 fusion.113
  276.7 14.2 %all_gather.65 = bf16[1536,256]{1,0:T(8,128)(2,1)S(1)} all-gather(bf16[192,256]{1,0:T(8,128)(2,1)S(1)} %get-tuple-element.58), channel_id=1, replica_groups=mesh['section'=2,'seq'=8,'wa'=8] {'wa'}, dimensions={0}, use_global_device_ids=true | all-gather | bytes 884736 | tf_op jit(solution)/shard_map/all_gather | solution.py:368
  290.8 2.6 convolution_convert_fusion.1.do_ref
  293.4 4.8 attention_backward.2
  298.2 7.1 %all-to-all-start.6 = ((bf16[8,128,256]{2,1,0:T(8,128)(2,1)}), bf16[8,128,256]{2,1,0:T(8,128)(2,1)S(1)}, u32[]{:S(2)}, u32[]{:S(2)}) async-start(bf16[8,128,256]{2,1,0:T(8,128)(2,1)} %get-tuple-element.40), calls=%async_computation.6 | async-start | bytes 1048576 | tf_op jit(solution)/shard_map/all_to_all | solution.py:344
  306.3 9.6 %all-to-all-done.6 = bf16[8,128,256]{2,1,0:T(8,128)(2,1)S(1)} async-done(((bf16[8,128,256]{2,1,0:T(8,128)(2,1)}), bf16[8,128,256]{2,1,0:T(8,128)(2,1)S(1)}, u32[]{:S(2)}, u32[]{:S(2)}) %all-to-all-start.6) | async-done | bytes 524320 | tf_op jit(solution)/shard_map/all_to_all | solution.py:344
  317.0 22.6 %all-gather.14.cloned.1.call-done = bf16[2688,256]{1,0:T(8,128)(2,1)} async-done(((bf16[336,256]{1,0:T(8,128)(2,1)}), bf16[2688,256]{1,0:T(8,128)(2,1)}) %all-gather.14.cloned.1.call-update) | async-done | bytes 1376272 | tf_op jit(solution)/shard_map/all_gather | solution.py:545
  341.8 2.3 fusion.111
  344.2 1.5 collective-permute-start.1
  345.7 4.7 collective-permute-done.1
  350.4 15.3 %all_gather.68.dz_ref = bf16[1536,256]{1,0:T(8,128)(2,1)} all-gather(bf16[192,256]{1,0:T(8,128)(2,1)S(1)} %collective-permute-done.1), channel_id=1, replica_groups=mesh['section'=2,'seq'=8,'wa'=8] {'wa'}, dimensions={0}, use_global_device_ids=true | all-gather | bytes 884736 | tf_op jit(solution)/shard_map/all_gather | solution.py:368
  365.7 20.0 %experts_backward.3 = (bf16[1536,256]{1,0:T(8,128)(2,1)}, f32[40,1,256]{2,1,0:T(1,128)}, bf16[128,2560]{1,0:T(8,128)(2,1)}) custom-call(bf16[1536,256]{1,0:T(8,128)(2,1)} %all_gather.68.dz_ref, bf16[2560,256]{1,0:T(8,128)(2,1)} %get-tuple-element.41.g_ref, bf16[2560,256]{1,0:T(8,128)(2,1)} %get-tuple-element.42.u_ref, f32[40,1,256]{2,1,0:T(1,128)} %copy.62.gate_ref, ...), custom_call_target="tpu_custom_call" | custom-call | flops 6039797760 | bytes 28000000 | tf_op jit(solution)/shard_map/experts_backward/pallas_call | solution.py:173
  385.8 1.5 multiply_reduce_fusion
  387.6 15.9 %all_to_all.65 = bf16[8,208,256]{2,1,0:T(8,128)(2,1)S(1)} all-to-all(bf16[8,208,256]{2,1,0:T(8,128)(2,1)S(1)} %pad_maximum_fusion.2), channel_id=1, replica_groups=mesh['section'=2,'seq'=8,'wa'=8] {'wa'}, dimensions={0} | all-to-all | bytes 1703936 | tf_op jit(solution)/shard_map/all_to_all | solution.py:344
  405.7 14.0 %all_gather.69 = bf16[1536,256]{1,0:T(8,128)(2,1)S(1)} all-gather(bf16[192,256]{1,0:T(8,128)(2,1)S(1)} %get-tuple-element.109), channel_id=1, replica_groups=mesh['section'=2,'seq'=8,'wa'=8] {'wa'}, dimensions={0}, use_global_device_ids=true | all-gather | bytes 884736 | tf_op jit(solution)/shard_map/all_gather | solution.py:368
  419.7 2.6 convolution_convert_fusion.do_ref
  422.3 4.8 attention_backward.3
  427.1 6.6 all-to-all-start.8
  435.2 9.0 %all-to-all-done.8 = bf16[8,128,256]{2,1,0:T(8,128)(2,1)S(1)} async-done(((bf16[8,128,256]{2,1,0:T(8,128)(2,1)}), bf16[8,128,256]{2,1,0:T(8,128)(2,1)S(1)}, u32[]{:S(2)}, u32[]{:S(2)}) %all-to-all-start.8) | async-done | bytes 524320 | tf_op jit(solution)/shard_map/all_to_all | solution.py:344
  448.1 2.0 broadcast_select_fusion.2
  450.2 5.4 all-to-all-start.4
  456.2 28.3 %all_gather.74 = bf16[8,40,256]{2,1,0:T(8,128)(2,1)S(1)} all-gather(bf16[1,40,256]{2,1,0:T(8,128)(2,1)S(1)} %pad_maximum_fusion.17), channel_id=1, replica_groups=mesh['section'=2,'seq'=8,'wa'=8] {'seq'}, dimensions={0}, use_global_device_ids=true | all-gather | bytes 184320 | tf_op jit(solution)/shard_map/all_gather | solution.py:414
  486.8 1.6 bitcast_bitcast_fusion.1
  489.4 1.6 fusion.117
  492.1 4.2 all-to-all-start.12
  496.3 2.4 fusion.17
  498.7 2.4 reshape.546
  501.2 2.2 copy.94
  505.5 1.8 fusion.28
  507.2 1.5 slice.334
  512.8 2.4 fusion.4
  515.2 7.0 %all-to-all-start.10 = ((bf16[8,192,192]{2,1,0:T(8,128)(2,1)}), bf16[8,192,192]{2,1,0:T(8,128)(2,1)S(1)}, u32[]{:S(2)}, u32[]{:S(2)}) async-start(bf16[8,192,192]{2,1,0:T(8,128)(2,1)} %bitcast.264), calls=%async_computation.10 | async-start | bytes 1572864 | tf_op jit(solution)/shard_map/all_to_all | solution.py:344
  525.5 9.7 %all-to-all-done.10 = bf16[8,192,192]{2,1,0:T(8,128)(2,1)S(1)} async-done(((bf16[8,192,192]{2,1,0:T(8,128)(2,1)}), bf16[8,192,192]{2,1,0:T(8,128)(2,1)S(1)}, u32[]{:S(2)}, u32[]{:S(2)}) %all-to-all-start.10) | async-done | bytes 589856 | tf_op jit(solution)/shard_map/all_to_all | solution.py:344
  535.2 5.7 all-to-all-start.9
  540.9 12.2 %expert_weight_grad.3 = f32[40,64,192]{2,1,0:T(8,128)} custom-call(bf16[8,64,2560]{2,1,0:T(8,128)(2,1)} %bitcast.337, bf16[8,192,256]{2,1,0:T(8,128)(2,1)} %all-to-all-done.12.feature_ref, f32[8,40,1,256]{3,2,1,0:T(1,128)} %reshape.550.place_ref), custom_call_target="tpu_custom_call" | custom-call | flops 4026531840 | bytes 15000000 | tf_op jit(solution)/shard_map/expert_weight_grad/pallas_call | solution.py:216
  554.0 35.5 %psum.7 = f32[192,41]{0,1:T(8,128)S(1)} all-reduce(f32[192,41]{0,1:T(8,128)S(1)} %pad_maximum_fusion.15), channel_id=1, replica_groups=mesh['section'=2,'seq'=8,'wa'=8] {'seq'}, use_global_device_ids=true, to_apply=%region_33.34 | all-reduce | flops 7872 | bytes 62976 | tf_op jit(solution)/shard_map/psum | solution.py:596
  590.1 3.5 all-to-all-start.11
  596.1 8.7 %all-to-all-done.11.feature_ref = bf16[8,192,256]{2,1,0:T(8,128)(2,1)S(1)} async-done(((bf16[8,192,256]{2,1,0:T(8,128)(2,1)}), bf16[8,192,256]{2,1,0:T(8,128)(2,1)S(1)}, u32[]{:S(2)}, u32[]{:S(2)}) %all-to-all-start.11) | async-done | bytes 786464 | tf_op jit(solution)/shard_map/all_to_all | solution.py:344
  604.8 26.3 %all-gather.18.cloned.1.call-done = bf16[1024,2560]{1,0:T(8,128)(2,1)} async-done(((bf16[128,2560]{1,0:T(8,128)(2,1)}), bf16[1024,2560]{1,0:T(8,128)(2,1)}) %all-gather.18.cloned.1.call-update) | async-done | bytes 5242896 | tf_op jit(solution)/shard_map/all_gather | solution.py:591
  631.1 19.9 %expert_weight_grad.2 = f32[40,128,192]{2,1,0:T(8,128)} custom-call(bf16[8,128,2560]{2,1,0:T(8,128)(2,1)} %bitcast.336, bf16[8,192,256]{2,1,0:T(8,128)(2,1)} %copy-done.38, f32[8,40,1,256]{3,2,1,0:T(1,128)} %reshape.550.place_ref), custom_call_target="tpu_custom_call" | custom-call | flops 8053063680 | bytes 15000000 | tf_op jit(solution)/shard_map/expert_weight_grad/pallas_call | solution.py:216
  (407 shorter events, 56.1 us)
Async XLA Ops:
  7.2 100.0 %all-gather.12.cloned.1.call-start = ((), (), s32[]{:S(2)}) async-start(), calls=%async_computation.13 | async-start | bytes 5308416 | tf_op jit(solution)/shard_map/all_gather | solution.py:368
  11.1 54.3 %all-to-all-start = ((bf16[8,192,320]{2,1,0:T(8,128)(2,1)}), bf16[8,192,320]{2,1,0:T(8,128)(2,1)S(1)}, u32[]{:S(2)}, u32[]{:S(2)}) async-start(bf16[8,192,320]{2,1,0:T(8,128)(2,1)} %bitcast.242), calls=%async_computation | async-start | bytes 2359296 | tf_op jit(solution)/shard_map/all_to_all | solution.py:344
  18.5 31.7 %copy-start.40 = (bf16[192,128]{1,0:T(8,128)(2,1)}, bf16[192,128]{1,0:T(8,128)(2,1)S(1)}, u32[]{:S(2)}) copy-start(bf16[192,128]{1,0:T(8,128)(2,1)S(1)} %get-tuple-element.78) | copy-start | bytes 147460
  18.5 31.7 %copy-start.42 = (bf16[192,128]{1,0:T(8,128)(2,1)}, bf16[192,128]{1,0:T(8,128)(2,1)S(1)}, u32[]{:S(2)}) copy-start(bf16[192,128]{1,0:T(8,128)(2,1)S(1)} %get-tuple-element.79) | copy-start | bytes 147460
  50.2 15.2 %copy-start.98 = (f32[256]{0:T(256)}, f32[256]{0:T(256)S(1)}, u32[]{:S(2)}) copy-start(f32[256]{0:T(256)S(1)} %fusion.18) | copy-start | bytes 3076
  50.2 15.2 %copy-start.85 = (f32[256]{0:T(256)}, f32[256]{0:T(256)S(1)}, u32[]{:S(2)}) copy-start(f32[256]{0:T(256)S(1)} %add_rsqrt_fusion.1) | copy-start | bytes 3076
  65.0 46.2 %copy-start.59 = (f32[1536]{0:T(1024)}, f32[1536]{0:T(1024)S(1)}, u32[]{:S(2)}) copy-start(f32[1536]{0:T(1024)S(1)} %get-tuple-element.52) | copy-start | bytes 18436
  67.1 18.5 %all-to-all-start.1 = ((bf16[8,128,256]{2,1,0:T(8,128)(2,1)}), bf16[8,128,256]{2,1,0:T(8,128)(2,1)S(1)}, u32[]{:S(2)}, u32[]{:S(2)}) async-start(bf16[8,128,256]{2,1,0:T(8,128)(2,1)} %broadcast_in_dim.167), calls=%async_computation.1 | async-start | bytes 1048576 | tf_op jit(solution)/shard_map/all_to_all | solution.py:344
  111.2 292.9 %copy-start.74 = (f32[256]{0:T(256)}, f32[256]{0:T(256)S(1)}, u32[]{:S(2)}) copy-start(f32[256]{0:T(256)S(1)} %fusion.100) | copy-start | bytes 3076
  112.3 18.2 %copy-start.24 = (f32[40,256]{1,0:T(8,128)}, f32[40,256]{1,0:T(8,128)S(1)}, u32[]{:S(2)}) copy-start(f32[40,256]{1,0:T(8,128)S(1)} %get-tuple-element.102) | copy-start | bytes 122884
  112.4 18.2 %copy-start.77 = (f32[256]{0:T(256)}, f32[256]{0:T(256)S(1)}, u32[]{:S(2)}) copy-start(f32[256]{0:T(256)S(1)} %get-tuple-element.62) | copy-start | bytes 3076
  112.4 18.1 %copy-start.82 = (f32[256]{0:T(256)}, f32[256]{0:T(256)S(1)}, u32[]{:S(2)}) copy-start(f32[256]{0:T(256)S(1)} %fusion.72) | copy-start | bytes 3076
  130.6 16.2 %all-to-all-start.2 = ((bf16[8,192,256]{2,1,0:T(8,128)(2,1)}), bf16[8,192,256]{2,1,0:T(8,128)(2,1)S(1)}, u32[]{:S(2)}, u32[]{:S(2)}) async-start(bf16[8,192,256]{2,1,0:T(8,128)(2,1)} %bitcast.282), calls=%async_computation.2 | async-start | bytes 1572864 | tf_op jit(solution)/shard_map/all_to_all | solution.py:344
  146.8 20.1 %copy-start.71 = (f32[1536]{0:T(1024)S(1)}, f32[1536]{0:T(1024)}, u32[]{:S(2)}) copy-start(f32[1536]{0:T(1024)} %copy-done.70) | copy-start | bytes 18436
  146.9 20.2 %copy-start.49 = (bf16[192,256]{1,0:T(8,128)(2,1)}, bf16[192,256]{1,0:T(8,128)(2,1)S(1)}, u32[]{:S(2)}) copy-start(bf16[192,256]{1,0:T(8,128)(2,1)S(1)} %add_convert_fusion.1) | copy-start | bytes 294916
  147.0 4.6 collective-permute-start
  150.7 123.2 %copy-start.62 = (s32[8,256]{1,0:T(8,128)}, s32[8,256]{1,0:T(8,128)S(1)}, u32[]{:S(2)}) copy-start(s32[8,256]{1,0:T(8,128)S(1)} %pad_add_fusion) | copy-start | bytes 24580
  151.6 190.2 %copy-start.28 = (bf16[192,256]{1,0:T(8,128)(2,1)}, bf16[192,256]{1,0:T(8,128)(2,1)S(1)}, u32[]{:S(2)}) copy-start(bf16[192,256]{1,0:T(8,128)(2,1)S(1)} %collective-permute-done) | copy-start | bytes 294916
  169.0 19.5 %all-to-all-start.3 = ((bf16[8,128,256]{2,1,0:T(8,128)(2,1)}), bf16[8,128,256]{2,1,0:T(8,128)(2,1)S(1)}, u32[]{:S(2)}, u32[]{:S(2)}) async-start(bf16[8,128,256]{2,1,0:T(8,128)(2,1)} %broadcast_in_dim.176), calls=%async_computation.3 | async-start | bytes 1048576 | tf_op jit(solution)/shard_map/all_to_all | solution.py:344
  173.0 80.9 %copy-start.113 = (bf16[16]{0:T(256)(128)(2,1)}, bf16[16]{0:T(256)(128)(2,1)S(1)}, u32[]{:S(2)}) copy-start(bf16[16]{0:T(256)(128)(2,1)S(1)} %pad.44.clone) | copy-start | bytes 100
  212.3 61.9 %copy-start.3 = (f32[1536,256]{1,0:T(8,128)}, f32[1536,256]{1,0:T(8,128)S(1)}, u32[]{:S(2)}) copy-start(f32[1536,256]{1,0:T(8,128)S(1)} %get-tuple-element.104) | copy-start | bytes 4718596
  212.4 61.9 %copy-start.84 = (f32[256]{0:T(256)}, f32[256]{0:T(256)S(1)}, u32[]{:S(2)}) copy-start(f32[256]{0:T(256)S(1)} %fusion.101) | copy-start | bytes 3076
  255.0 19.0 %copy-start.46 = (bf16[1,192,40]{1,2,0:T(8,128)(2,1)S(1)}, bf16[1,192,40]{1,2,0:T(8,128)(2,1)}, u32[]{:S(2)}) copy-start(bf16[1,192,40]{1,2,0:T(8,128)(2,1)} %param.15) | copy-start | bytes 46084
  255.0 17.5 %all-to-all-start.5 = ((bf16[8,208,256]{2,1,0:T(8,128)(2,1)}), bf16[8,208,256]{2,1,0:T(8,128)(2,1)}, u32[]{:S(2)}, u32[]{:S(2)}) async-start(bf16[8,208,256]{2,1,0:T(8,128)(2,1)} %pad_maximum_fusion.1), calls=%async_computation.5 | async-start | bytes 1703936 | tf_op jit(solution)/shard_map/all_to_all | solution.py:344
  274.0 19.5 %copy-start.26 = (f32[40,256]{1,0:T(8,128)}, f32[40,256]{1,0:T(8,128)S(1)}, u32[]{:S(2)}) copy-start(f32[40,256]{1,0:T(8,128)S(1)} %get-tuple-element.61) | copy-start | bytes 122884
  276.0 65.8 %copy-start.18 = (f32[192,256]{1,0:T(8,128)}, f32[192,256]{1,0:T(8,128)S(1)}, u32[]{:S(2)}) copy-start(f32[192,256]{1,0:T(8,128)S(1)} %get-tuple-element.59) | copy-start | bytes 589828
  290.8 14.6 %copy-start.58 = (f32[32,2,128]{2,1,0:T(2,128)S(1)}, f32[32,2,128]{2,1,0:T(2,128)}, u32[]{:S(2)}) copy-start(f32[32,2,128]{2,1,0:T(2,128)} %copy-done.57) | copy-start | bytes 98308
  293.4 22.5 %copy-start.21 = (bf16[3,64,256]{2,1,0:T(8,128)(2,1)S(1)}, bf16[3,64,256]{2,1,0:T(8,128)(2,1)}, u32[]{:S(2)}) copy-start(bf16[3,64,256]{2,1,0:T(8,128)(2,1)} %pad_maximum_fusion.7) | copy-start | bytes 294916
  298.2 17.7 %copy-start.44 = (f32[192,256]{1,0:T(8,128)S(1)}, f32[192,256]{1,0:T(8,128)}, u32[]{:S(2)}) copy-start(f32[192,256]{1,0:T(8,128)} %get-tuple-element.39) | copy-start | bytes 589828
  298.2 17.6 %all-to-all-start.6 = ((bf16[8,128,256]{2,1,0:T(8,128)(2,1)}), bf16[8,128,256]{2,1,0:T(8,128)(2,1)S(1)}, u32[]{:S(2)}, u32[]{:S(2)}) async-start(bf16[8,128,256]{2,1,0:T(8,128)(2,1)} %get-tuple-element.40), calls=%async_computation.6 | async-start | bytes 1048576 | tf_op jit(solution)/shard_map/all_to_all | solution.py:344
  305.3 34.3 %all-gather.14.cloned.1.call-start = ((), (), s32[]{:S(2)}) async-start(), calls=%async_computation.14 | async-start | bytes 1548288 | tf_op jit(solution)/shard_map/all_gather | solution.py:545
  305.4 11.5 %copy-start.94 = (bf16[336]{0:T(512)(128)(2,1)}, bf16[336]{0:T(512)(128)(2,1)S(1)}, u32[]{:S(2)}) copy-start(bf16[336]{0:T(512)(128)(2,1)S(1)} %pad.31.clone) | copy-start | bytes 2020
  305.5 11.6 %copy-start.53 = (f32[32,256]{1,0:T(8,128)}, f32[32,256]{1,0:T(8,128)S(1)}, u32[]{:S(2)}) copy-start(f32[32,256]{1,0:T(8,128)S(1)} %fusion.108) | copy-start | bytes 98308
  316.2 25.6 %copy-start.101 = (f32[256]{0:T(256)S(1)}, f32[256]{0:T(256)}, u32[]{:S(2)}) copy-start(f32[256]{0:T(256)} %copy-done.100) | copy-start | bytes 3076
  316.2 25.6 %copy-start.88 = (f32[256]{0:T(256)S(1)}, f32[256]{0:T(256)}, u32[]{:S(2)}) copy-start(f32[256]{0:T(256)} %copy-done.87) | copy-start | bytes 3076
  316.2 25.6 %copy-start.96 = (f32[1,1,192]{2,1,0:T(1,128)S(1)}, f32[1,1,192]{2,1,0:T(1,128)}, u32[]{:S(2)}) copy-start(f32[1,1,192]{2,1,0:T(1,128)} %get-tuple-element.96) | copy-start | bytes 2308
  341.8 24.0 %copy-start.90 = (f32[256]{0:T(256)}, f32[256]{0:T(256)S(1)}, u32[]{:S(2)}) copy-start(f32[256]{0:T(256)S(1)} %fusion.92) | copy-start | bytes 3076
  344.2 6.2 collective-permute-start.1
  350.4 53.7 %copy-start.32 = (bf16[192,256]{1,0:T(8,128)(2,1)}, bf16[192,256]{1,0:T(8,128)(2,1)S(1)}, u32[]{:S(2)}) copy-start(bf16[192,256]{1,0:T(8,128)(2,1)S(1)} %collective-permute-done.1) | copy-start | bytes 294916
  365.7 20.0 %copy-start.61 = (f32[1536]{0:T(1024)S(1)}, f32[1536]{0:T(1024)}, u32[]{:S(2)}) copy-start(f32[1536]{0:T(1024)} %copy-done.59) | copy-start | bytes 18436
  387.6 16.1 %copy-start.25 = (f32[40,256]{1,0:T(8,128)S(1)}, f32[40,256]{1,0:T(8,128)}, u32[]{:S(2)}) copy-start(f32[40,256]{1,0:T(8,128)} %copy-done.24) | copy-start | bytes 122884
  387.6 16.1 %copy-start.78 = (f32[256]{0:T(256)S(1)}, f32[256]{0:T(256)}, u32[]{:S(2)}) copy-start(f32[256]{0:T(256)} %copy-done.77) | copy-start | bytes 3076
  387.6 16.1 %copy-start.83 = (f32[256]{0:T(256)S(1)}, f32[256]{0:T(256)}, u32[]{:S(2)}) copy-start(f32[256]{0:T(256)} %copy-done.82) | copy-start | bytes 3076
  387.6 16.2 %copy-start.112 = (f32[256]{0:T(256)S(1)}, f32[256]{0:T(256)}, u32[]{:S(2)}) copy-start(f32[256]{0:T(256)} %copy-done.111) | copy-start | bytes 3076
  387.6 16.5 %copy-start.80 = (f32[1,1,192]{2,1,0:T(1,128)S(1)}, f32[1,1,192]{2,1,0:T(1,128)}, u32[]{:S(2)}) copy-start(f32[1,1,192]{2,1,0:T(1,128)} %get-tuple-element.97) | copy-start | bytes 2308
  403.8 18.5 %copy-start.22 = (f32[40,256]{1,0:T(8,128)}, f32[40,256]{1,0:T(8,128)S(1)}, u32[]{:S(2)}) copy-start(f32[40,256]{1,0:T(8,128)S(1)} %get-tuple-element.57) | copy-start | bytes 122884
  404.1 15.6 %copy-start.92 = (f32[1,256]{1,0:T(1,128)}, f32[1,256]{1,0:T(1,128)S(1)}, u32[]{:S(2)}) copy-start(f32[1,256]{1,0:T(1,128)S(1)} %fusion.98) | copy-start | bytes 3076
  422.3 22.0 %copy-start.20 = (bf16[3,64,256]{2,1,0:T(8,128)(2,1)S(1)}, bf16[3,64,256]{2,1,0:T(8,128)(2,1)}, u32[]{:S(2)}) copy-start(bf16[3,64,256]{2,1,0:T(8,128)(2,1)} %pad_maximum_fusion.8) | copy-start | bytes 294916
  427.1 17.1 %all-to-all-start.8 = ((bf16[8,128,256]{2,1,0:T(8,128)(2,1)}), bf16[8,128,256]{2,1,0:T(8,128)(2,1)S(1)}, u32[]{:S(2)}, u32[]{:S(2)}) async-start(bf16[8,128,256]{2,1,0:T(8,128)(2,1)} %get-tuple-element.47), calls=%async_computation.8 | async-start | bytes 1048576 | tf_op jit(solution)/shard_map/all_to_all | solution.py:344
  433.7 12.8 %copy-start.95 = (bf16[336]{0:T(512)(128)(2,1)S(1)}, bf16[336]{0:T(512)(128)(2,1)}, u32[]{:S(2)}) copy-start(bf16[336]{0:T(512)(128)(2,1)} %copy-done.94) | copy-start | bytes 2020
  433.7 73.6 %all-gather.16.cloned.1.call-start = ((), (), s32[]{:S(2)}) async-start(), calls=%async_computation.15 | async-start | bytes 1548288 | tf_op jit(solution)/shard_map/all_gather | solution.py:545
  447.2 93.6 %all-gather.20.cloned.1.call-start = ((), (), s32[]{:S(2)}) async-start(), calls=%async_computation.17 | async-start | bytes 2949120 | tf_op jit(solution)/shard_map/all_gather | solution.py:580
  448.1 183.0 %all-gather.18.cloned.1.call-start = ((), (), s32[]{:S(2)}) async-start(), calls=%async_computation.16 | async-start | bytes 5898240 | tf_op jit(solution)/shard_map/all_gather | solution.py:591
  450.2 36.6 %copy-start.50 = (bf16[192,256]{1,0:T(8,128)(2,1)S(1)}, bf16[192,256]{1,0:T(8,128)(2,1)}, u32[]{:S(2)}) copy-start(bf16[192,256]{1,0:T(8,128)(2,1)} %copy-done.49) | copy-start | bytes 294916
  450.2 38.2 %copy-start.27 = (f32[40,256]{1,0:T(8,128)S(1)}, f32[40,256]{1,0:T(8,128)}, u32[]{:S(2)}) copy-start(f32[40,256]{1,0:T(8,128)} %copy-done.26) | copy-start | bytes 122884
  450.2 35.2 %all-to-all-start.4 = ((bf16[8,192,256]{2,1,0:T(8,128)(2,1)}), bf16[8,192,256]{2,1,0:T(8,128)(2,1)}, u32[]{:S(2)}, u32[]{:S(2)}) async-start(bf16[8,192,256]{2,1,0:T(8,128)(2,1)} %bitcast.281), calls=%async_computation.4 | async-start | bytes 1572864 | tf_op jit(solution)/shard_map/all_to_all | solution.py:344
  492.1 23.2 %all-to-all-start.12 = ((bf16[8,192,256]{2,1,0:T(8,128)(2,1)}), bf16[8,192,256]{2,1,0:T(8,128)(2,1)}, u32[]{:S(2)}, u32[]{:S(2)}) async-start(bf16[8,192,256]{2,1,0:T(8,128)(2,1)} %bitcast.263), calls=%async_computation.12 | async-start | bytes 1572864 | tf_op jit(solution)/shard_map/all_to_all | solution.py:344
  515.2 20.0 %all-to-all-start.10 = ((bf16[8,192,192]{2,1,0:T(8,128)(2,1)}), bf16[8,192,192]{2,1,0:T(8,128)(2,1)S(1)}, u32[]{:S(2)}, u32[]{:S(2)}) async-start(bf16[8,192,192]{2,1,0:T(8,128)(2,1)} %bitcast.264), calls=%async_computation.10 | async-start | bytes 1572864 | tf_op jit(solution)/shard_map/all_to_all | solution.py:344
  535.2 54.9 %all-to-all-start.9 = ((bf16[8,192,384]{2,1,0:T(8,128)(2,1)}), bf16[8,192,384]{2,1,0:T(8,128)(2,1)S(1)}, u32[]{:S(2)}, u32[]{:S(2)}) async-start(bf16[8,192,384]{2,1,0:T(8,128)(2,1)} %pad_maximum_fusion), calls=%async_computation.9 | async-start | bytes 2359296 | tf_op jit(solution)/shard_map/all_to_all | solution.py:344
  540.9 13.1 %copy-start.104 = (f32[192]{0:T(256)S(1)}, f32[192]{0:T(256)}, u32[]{:S(2)}) copy-start(f32[192]{0:T(256)} %get-tuple-element.64) | copy-start | bytes 2308
  540.9 13.1 %copy-start.64 = (f32[192,40]{0,1:T(8,128)S(1)}, f32[192,40]{0,1:T(8,128)}, u32[]{:S(2)}) copy-start(f32[192,40]{0,1:T(8,128)} %fusion.28) | copy-start | bytes 92164
  553.1 40.6 %copy-start.37 = (f32[24,2,8,128]{3,2,1,0:T(8,128)S(1)}, f32[24,2,8,128]{3,2,1,0:T(8,128)}, u32[]{:S(2)}) copy-start(f32[24,2,8,128]{3,2,1,0:T(8,128)} %get-tuple-element.66) | copy-start | bytes 589828
  590.1 14.7 %all-to-all-start.11 = ((bf16[8,192,256]{2,1,0:T(8,128)(2,1)}), bf16[8,192,256]{2,1,0:T(8,128)(2,1)S(1)}, u32[]{:S(2)}, u32[]{:S(2)}) async-start(bf16[8,192,256]{2,1,0:T(8,128)(2,1)} %bitcast.96), calls=%async_computation.11 | async-start | bytes 1572864 | tf_op jit(solution)/shard_map/all_to_all | solution.py:344
  604.8 26.3 %copy-start.38 = (bf16[8,192,256]{2,1,0:T(8,128)(2,1)}, bf16[8,192,256]{2,1,0:T(8,128)(2,1)S(1)}, u32[]{:S(2)}) copy-start(bf16[8,192,256]{2,1,0:T(8,128)(2,1)S(1)} %all-to-all-done.11.feature_ref) | copy-start | bytes 2359300
  (71 other events, 161.0 us)
Sparse Core Ops, SparseCore 0:
  9.7 48.4 all-gather.11
  317.1 22.3 all-gather.13
  447.4 23.2 all-gather.15
  472.8 64.4 all-gather.19
  539.5 91.5 all-gather.17

commit v2 on v1

--- a/solution.py
+++ b/solution.py
@@ -23,14 +23,16 @@
 HIDDEN = 64
 SLOTS = MICRO * CAP
 GROUP_COLS = (PER_GROUP + 2) * HEAD_DIM
-BATCH = 4
-STEPS = EXPERTS // BATCH
-BLOCK = BATCH * HIDDEN
+QUAD = 4
+COLUMNS = 256
+FORWARD_CHUNKS = (8, 16, 16)
+BACKWARD_CHUNKS = (8, 16, 16)
 SCALE = HEAD_DIM ** (-0.5)
 EPSILON = 1e-06
 BF16 = jnp.bfloat16
 F32 = jnp.float32
-VMEM_LIMIT = 56 * 1024 * 1024
+VMEM_LIMIT = 20 * 1024 * 1024
+EXPERT_VMEM = 48 * 1024 * 1024
 
 
 def dot_nn(a, b):
@@ -52,183 +54,239 @@
 
 
 def one_hot_slots(places):
-    slot = lax.broadcasted_iota(jnp.int32, (BATCH, SLOTS, TOKENS), 1).astype(F32)
+    slot = lax.broadcasted_iota(jnp.int32, (QUAD, SLOTS, TOKENS), 1).astype(F32)
     hit = jnp.where(slot == places, 1.0, 0.0)
-    return hit.reshape(BATCH * SLOTS, TOKENS).astype(BF16)
-
-
-def own_slots(rows, pick, height):
-    every = dot_nt(rows, pick)
-    lane = lax.broadcasted_iota(jnp.int32, (height, BATCH * SLOTS), 1) // SLOTS
-    out = every[:height]
-    for e in range(1, BATCH):
-        out = jnp.where(lane == e, every[e * height : (e + 1) * height], out)
-    return out.astype(BF16)
-
-
-def spread_slots(compact):
-    lane = lax.broadcasted_iota(jnp.int32, compact.shape, 1) // SLOTS
-    zero = jnp.zeros_like(compact)
-    return jnp.concatenate([jnp.where(lane == e, compact, zero) for e in range(BATCH)], axis=0)
+    return hit.reshape(QUAD * SLOTS, TOKENS).astype(BF16)
+
+
+def chunk_starts(chunks):
+    return [sum(chunks[:c]) for c in range(len(chunks))]
+
+
+def copies_in(sources, targets, sems, order, chunks):
+    copies = [[] for _ in sources]
+    for c, (first, size) in enumerate(zip(chunk_starts(chunks), chunks)):
+        for k in order:
+            rows = sources[k].shape[0] // EXPERTS
+            part = pl.ds(first * rows, size * rows)
+            copy = pltpu.make_async_copy(sources[k].at[part], targets[k].at[part], sems.at[k, c])
+            copy.start()
+            copies[k].append(copy)
+    return copies
+
+
+def accumulate(first, total, left, right_ref):
+    for c in range(0, WIDTH, COLUMNS):
+        cols = slice(c, c + COLUMNS)
+        part = dot_tn(right_ref[..., cols].reshape(left.shape[0], COLUMNS), left)
+        if first:
+            total[cols] = part
+        else:
+            total[cols] += part
 
 
 def experts_forward_kernel(
-    x_ref, gate_ref, place_ref, win_ref, wout_ref, y_ref, g_ref, u_ref, f_ref, total
+    x_ref, gate_ref, place_ref, win_hbm, wout_hbm,
+    y_ref, f_ref, g_hbm, u_hbm,
+    win, wout, g_all, u_all, total, in_sems, out_sems,
 ):
-    step = pl.program_id(0)
-    x = x_ref[...]
-    wg = win_ref[:, 0].reshape(BLOCK, WIDTH)
-    wu = win_ref[:, 1].reshape(BLOCK, WIDTH)
-    g = dot_nn(wg, x)
-    u = dot_nn(wu, x)
-    g_ref[...] = g.astype(BF16)
-    u_ref[...] = u.astype(BF16)
-    active = (g * jax.nn.sigmoid(g) * u).astype(BF16).astype(F32)
-    gated = (active.reshape(BATCH, HIDDEN, TOKENS) * gate_ref[...]).astype(BF16)
-    gated = gated.reshape(BLOCK, TOKENS)
-    f_ref[...] = own_slots(gated, one_hot_slots(place_ref[...]), HIDDEN)
-    part = dot_tn(gated, wout_ref[...].reshape(BLOCK, WIDTH))
-
-    @pl.when(step == 0)
-    def _():
-        total[...] = part
-
-    @pl.when(step > 0)
-    def _():
-        total[...] += part
-
-    @pl.when(step == STEPS - 1)
-    def _():
-        y_ref[...] = total[...].astype(BF16).T
+    arriving = copies_in((win_hbm, wout_hbm), (win, wout), in_sems, (0, 1), FORWARD_CHUNKS)
+    leaving = []
+    lane = lax.broadcasted_iota(jnp.int32, (SLOTS, 2 * HIDDEN), 1)
+    for c, (first, size) in enumerate(zip(chunk_starts(FORWARD_CHUNKS), FORWARD_CHUNKS)):
+        block = size * HIDDEN
+        some = pl.ds(first, size)
+        rows = pl.ds(first * HIDDEN, block)
+        arriving[0][c].wait()
+        g = dot_nn(win[some, 0].reshape(block, WIDTH), x_ref[...])
+        u = dot_nn(win[some, 1].reshape(block, WIDTH), x_ref[...])
+        g_all[rows] = g.astype(BF16)
+        u_all[rows] = u.astype(BF16)
+        for k, (vmem, hbm) in enumerate(((g_all, g_hbm), (u_all, u_hbm))):
+            copy = pltpu.make_async_copy(vmem.at[rows], hbm.at[rows], out_sems.at[k, c])
+            copy.start()
+            leaving.append(copy)
+        active = (g * jax.nn.sigmoid(g) * u).astype(BF16).astype(F32)
+        gated = (active.reshape(size, HIDDEN, TOKENS) * gate_ref[some]).astype(BF16)
+        gated = gated.reshape(block, TOKENS)
+        for q in range(0, size, QUAD):
+            pick = one_hot_slots(place_ref[pl.ds(first + q, QUAD)])
+            every = dot_nt(pick, gated[q * HIDDEN : (q + QUAD) * HIDDEN])
+            for p in range(QUAD // 2):
+                lanes = slice(2 * p * HIDDEN, 2 * (p + 1) * HIDDEN)
+                even = every[2 * p * SLOTS : (2 * p + 1) * SLOTS, lanes]
+                odd = every[(2 * p + 1) * SLOTS : (2 * p + 2) * SLOTS, lanes]
+                row = ((first + q) // 2 + p) * SLOTS
+                f_ref[pl.ds(row, SLOTS)] = jnp.where(lane < HIDDEN, even, odd).astype(BF16)
+        arriving[1][c].wait()
+        accumulate(c == 0, total, gated, wout.at[some])
+    y_ref[...] = total[...].astype(BF16)
+    for copy in leaving:
+        copy.wait()
+
+
+def vmem_spec():
+    return pl.BlockSpec(memory_space=pltpu.VMEM)
+
+
+def any_spec():
+    return pl.BlockSpec(memory_space=pl.ANY)
+
+
+def expert_scratch():
+    return [
+        pltpu.VMEM((EXPERTS, 2, HIDDEN, WIDTH), BF16),
+        pltpu.VMEM((EXPERTS, HIDDEN, WIDTH), BF16),
+        pltpu.VMEM((EXPERTS * HIDDEN, TOKENS), BF16),
+        pltpu.VMEM((EXPERTS * HIDDEN, TOKENS), BF16),
+        pltpu.VMEM((WIDTH, TOKENS), F32),
+    ]
+
+
+def expert_cost():
+    return pl.CostEstimate(
+        flops=6 * TOKENS * EXPERTS * HIDDEN * WIDTH, bytes_accessed=28_000_000, transcendentals=0
+    )
 
 
 def experts_forward(x, gates, places, w_in, w_out):
+    hidden = jax.ShapeDtypeStruct((EXPERTS * HIDDEN, TOKENS), BF16)
     return pl.pallas_call(
         experts_forward_kernel,
-        grid=(STEPS,),
-        in_specs=[
-            pl.BlockSpec((WIDTH, TOKENS), lambda i: (0, 0)),
-            pl.BlockSpec((BATCH, 1, TOKENS), lambda i: (i, 0, 0)),
-            pl.BlockSpec((BATCH, 1, TOKENS), lambda i: (i, 0, 0)),
-            pl.BlockSpec((BATCH, 2, HIDDEN, WIDTH), lambda i: (i, 0, 0, 0)),
-            pl.BlockSpec((BATCH, HIDDEN, WIDTH), lambda i: (i, 0, 0)),
-        ],
-        out_specs=[
-            pl.BlockSpec((WIDTH, TOKENS), lambda i: (0, 0)),
-            pl.BlockSpec((BLOCK, TOKENS), lambda i: (i, 0)),
-            pl.BlockSpec((BLOCK, TOKENS), lambda i: (i, 0)),
-            pl.BlockSpec((HIDDEN, BATCH * SLOTS), lambda i: (0, i)),
-        ],
+        in_specs=[vmem_spec(), vmem_spec(), vmem_spec(), any_spec(), any_spec()],
+        out_specs=[vmem_spec(), vmem_spec(), any_spec(), any_spec()],
         out_shape=[
             jax.ShapeDtypeStruct((WIDTH, TOKENS), BF16),
-            jax.ShapeDtypeStruct((EXPERTS * HIDDEN, TOKENS), BF16),
-            jax.ShapeDtypeStruct((EXPERTS * HIDDEN, TOKENS), BF16),
-            jax.ShapeDtypeStruct((HIDDEN, EXPERTS * SLOTS), BF16),
+            jax.ShapeDtypeStruct((EXPERTS // 2 * SLOTS, 2 * HIDDEN), BF16),
+            hidden,
+            hidden,
         ],
-        scratch_shapes=[pltpu.VMEM((TOKENS, WIDTH), F32)],
-        compiler_params=params(),
-        cost_estimate=pl.CostEstimate(
-            flops=6 * TOKENS * EXPERTS * HIDDEN * WIDTH, bytes_accessed=28_000_000, transcendentals=0
-        ),
+        scratch_shapes=expert_scratch()
+        + [pltpu.SemaphoreType.DMA((2, len(FORWARD_CHUNKS)))] * 2,
+        compiler_params=pltpu.CompilerParams(vmem_limit_bytes=EXPERT_VMEM),
+        cost_estimate=expert_cost(),
         name="experts_forward",
     )(x, gates, places, w_in, w_out)
 
 
 def experts_backward_kernel(
-    dz_ref, g_ref, u_ref, gate_ref, place_ref, win_ref, wout_ref, dx_ref, dgate_ref, du_ref, total
+    dz_ref, gate_ref, place_ref, g_hbm, u_hbm, win_hbm, wout_hbm,
+    dx_ref, dgate_ref, du_ref,
+    win, wout, g_all, u_all, total, in_sems,
 ):
-    step = pl.program_id(0)
-    through = dot_nn(wout_ref[...].reshape(BLOCK, WIDTH), dz_ref[...])
-    g = g_ref[...].astype(F32)
-    u = u_ref[...].astype(F32)
-    sig = jax.nn.sigmoid(g)
-    silu = g * sig
-    active = (silu * u).astype(BF16).astype(F32)
-    dgate_ref[...] = jnp.sum(
-        (active * through).reshape(BATCH, HIDDEN, TOKENS), axis=1, keepdims=True
-    )
-    df = (through.reshape(BATCH, HIDDEN, TOKENS) * gate_ref[...]).reshape(BLOCK, TOKENS)
-    dg = (df * u * (sig * (1.0 + g * (1.0 - sig)))).astype(BF16)
-    du = (df * silu).astype(BF16)
-    pick = one_hot_slots(place_ref[...])
-    du_ref[:HIDDEN] = own_slots(dg, pick, HIDDEN)
-    du_ref[HIDDEN:] = own_slots(du, pick, HIDDEN)
-    part = dot_tn(dg, win_ref[:, 0].reshape(BLOCK, WIDTH))
-    part += dot_tn(du, win_ref[:, 1].reshape(BLOCK, WIDTH))
-
-    @pl.when(step == 0)
-    def _():
-        total[...] = part
-
-    @pl.when(step > 0)
-    def _():
-        total[...] += part
-
-    @pl.when(step == STEPS - 1)
-    def _():
-        dx_ref[...] = total[...].astype(BF16).T
+    arriving = copies_in(
+        (win_hbm, wout_hbm, g_hbm, u_hbm),
+        (win, wout, g_all, u_all),
+        in_sems,
+        (1, 2, 3, 0),
+        BACKWARD_CHUNKS,
+    )
+    for c, (first, size) in enumerate(zip(chunk_starts(BACKWARD_CHUNKS), BACKWARD_CHUNKS)):
+        block = size * HIDDEN
+        some = pl.ds(first, size)
+        rows = pl.ds(first * HIDDEN, block)
+        arriving[1][c].wait()
+        through = dot_nn(wout[some].reshape(block, WIDTH), dz_ref[...])
+        arriving[2][c].wait()
+        arriving[3][c].wait()
+        g = g_all[rows].astype(F32)
+        u = u_all[rows].astype(F32)
+        sig = jax.nn.sigmoid(g)
+        silu = g * sig
+        active = (silu * u).astype(BF16).astype(F32)
+        dgate_ref[some] = jnp.sum(
+            (active * through).reshape(size, HIDDEN, TOKENS), axis=1, keepdims=True
+        )
+        df = (through.reshape(size, HIDDEN, TOKENS) * gate_ref[some]).reshape(block, TOKENS)
+        dg = (df * u * (sig * (1.0 + g * (1.0 - sig)))).astype(BF16)
+        du = (df * silu).astype(BF16)
+        both = jnp.concatenate(
+            [dg.reshape(size, 1, HIDDEN, TOKENS), du.reshape(size, 1, HIDDEN, TOKENS)], axis=1
+        ).reshape(2 * block, TOKENS)
+        for q in range(0, size, QUAD):
+            pick = one_hot_slots(place_ref[pl.ds(first + q, QUAD)])
+            every = dot_nt(pick, both[2 * q * HIDDEN : 2 * (q + QUAD) * HIDDEN])
+            for e in range(QUAD):
+                du_ref[pl.ds((first + q + e) * SLOTS, SLOTS)] = every[
+                    e * SLOTS : (e + 1) * SLOTS, 2 * e * HIDDEN : 2 * (e + 1) * HIDDEN
+                ].astype(BF16)
+        arriving[0][c].wait()
+        accumulate(c == 0, total, both, win.at[some])
+    dx_ref[...] = total[...].astype(BF16)
 
 
 def experts_backward(dz, g, u, gates, places, w_in, w_out):
     return pl.pallas_call(
         experts_backward_kernel,
-        grid=(STEPS,),
-        in_specs=[
-            pl.BlockSpec((WIDTH, TOKENS), lambda i: (0, 0)),
-            pl.BlockSpec((BLOCK, TOKENS), lambda i: (i, 0)),
-            pl.BlockSpec((BLOCK, TOKENS), lambda i: (i, 0)),
-            pl.BlockSpec((BATCH, 1, TOKENS), lambda i: (i, 0, 0)),
-            pl.BlockSpec((BATCH, 1, TOKENS), lambda i: (i, 0, 0)),
-            pl.BlockSpec((BATCH, 2, HIDDEN, WIDTH), lambda i: (i, 0, 0, 0)),
-            pl.BlockSpec((BATCH, HIDDEN, WIDTH), lambda i: (i, 0, 0)),
-        ],
-        out_specs=[
-            pl.BlockSpec((WIDTH, TOKENS), lambda i: (0, 0)),
-            pl.BlockSpec((BATCH, 1, TOKENS), lambda i: (i, 0, 0)),
-            pl.BlockSpec((2 * HIDDEN, BATCH * SLOTS), lambda i: (0, i)),
-        ],
+        in_specs=[vmem_spec(), vmem_spec(), vmem_spec()] + [any_spec()] * 4,
+        out_specs=[vmem_spec(), vmem_spec(), vmem_spec()],
         out_shape=[
             jax.ShapeDtypeStruct((WIDTH, TOKENS), BF16),
             jax.ShapeDtypeStruct((EXPERTS, 1, TOKENS), F32),
-            jax.ShapeDtypeStruct((2 * HIDDEN, EXPERTS * SLOTS), BF16),
+            jax.ShapeDtypeStruct((EXPERTS * SLOTS, 2 * HIDDEN), BF16),
         ],
-        scratch_shapes=[pltpu.VMEM((TOKENS, WIDTH), F32)],
-        compiler_params=params(),
-        cost_estimate=pl.CostEstimate(
-            flops=6 * TOKENS * EXPERTS * HIDDEN * WIDTH, bytes_accessed=28_000_000, transcendentals=0
-        ),
+        scratch_shapes=expert_scratch() + [pltpu.SemaphoreType.DMA((4, len(BACKWARD_CHUNKS)))],
+        compiler_params=pltpu.CompilerParams(vmem_limit_bytes=EXPERT_VMEM),
+        cost_estimate=expert_cost(),
         name="experts_backward",
-    )(dz, g, u, gates, places, w_in, w_out)
-
-
-def weight_grad_kernel(compact_ref, feature_ref, place_ref, out_ref):
-    height = compact_ref.shape[1]
-    total = jnp.zeros((BATCH * height, OWN), F32)
+    )(dz, gates, places, g, u, w_in, w_out)
+
+
+def slot_rows(feature_ref, place_ref):
+    rows = []
     for s in range(N_SEQ):
-        pick = one_hot_slots(place_ref[s])
-        rows = dot_nt(feature_ref[s], pick).astype(BF16)
-        total += dot_nt(spread_slots(compact_ref[s]), rows)
-    out_ref[...] = total.reshape(BATCH, height, OWN)
-
-
-def weight_grad(compact, feature, places):
-    height = compact.shape[1]
+        rows.append(dot_nt(one_hot_slots(place_ref[s]), feature_ref[s]).astype(BF16))
+    return [
+        jnp.concatenate([r[e * SLOTS : (e + 1) * SLOTS] for r in rows], axis=0)
+        for e in range(QUAD)
+    ]
+
+
+def weight_grad_in_kernel(compact_ref, feature_ref, place_ref, out_ref):
+    rows = slot_rows(feature_ref, place_ref)
+    for e in range(QUAD):
+        left = jnp.concatenate(
+            [compact_ref[s, e * SLOTS : (e + 1) * SLOTS] for s in range(N_SEQ)], axis=0
+        )
+        out_ref[e] = dot_tn(left, rows[e])
+
+
+def weight_grad_out_kernel(compact_ref, feature_ref, place_ref, out_ref):
+    rows = slot_rows(feature_ref, place_ref)
+    for p in range(QUAD // 2):
+        left = jnp.concatenate(
+            [compact_ref[s, p * SLOTS : (p + 1) * SLOTS] for s in range(N_SEQ)], axis=0
+        )
+        out_ref[2 * p] = dot_tn(left, rows[2 * p])[:HIDDEN]
+        out_ref[2 * p + 1] = dot_tn(left, rows[2 * p + 1])[HIDDEN:]
+
+
+def weight_grad(kernel, compact, feature, places, height):
+    block = compact.shape[1] * QUAD // EXPERTS
     return pl.pallas_call(
-        weight_grad_kernel,
-        grid=(STEPS,),
+        kernel,
+        grid=(EXPERTS // QUAD,),
         in_specs=[
-            pl.BlockSpec((N_SEQ, height, BATCH * SLOTS), lambda i: (0, 0, i)),
+            pl.BlockSpec((N_SEQ, block, 2 * HIDDEN), lambda i: (0, i, 0)),
             pl.BlockSpec((N_SEQ, OWN, TOKENS), lambda i: (0, 0, 0)),
-            pl.BlockSpec((N_SEQ, BATCH, 1, TOKENS), lambda i: (0, i, 0, 0)),
+            pl.BlockSpec((N_SEQ, QUAD, 1, TOKENS), lambda i: (0, i, 0, 0)),
         ],
-        out_specs=pl.BlockSpec((BATCH, height, OWN), lambda i: (i, 0, 0)),
+        out_specs=pl.BlockSpec((QUAD, height, OWN), lambda i: (i, 0, 0)),
         out_shape=jax.ShapeDtypeStruct((EXPERTS, height, OWN), F32),
         compiler_params=params(),
         cost_estimate=pl.CostEstimate(
-            flops=4 * N_SEQ * TOKENS * EXPERTS * height * OWN, bytes_accessed=15_000_000, transcendentals=0
+            flops=2 * N_SEQ * TOKENS * EXPERTS * SLOTS * OWN, bytes_accessed=15_000_000, transcendentals=0
         ),
         name="expert_weight_grad",
     )(compact, feature, places)
+
+
+def weight_grad_in(compact, feature, places):
+    return weight_grad(weight_grad_in_kernel, compact, feature, places, 2 * HIDDEN)
+
+
+def weight_grad_out(compact, feature, places):
+    return weight_grad(weight_grad_out_kernel, compact, feature, places, HIDDEN)
 
 
 def causal_mask(first):
@@ -340,6 +398,10 @@
     return high, (values - high.astype(F32)).astype(BF16)
 
 
+def after(value, *others):
+    return lax.optimization_barrier((value,) + others)[0]
+
+
 def exchange(blocks, axis):
     return lax.all_to_all(blocks, axis, split_axis=0, concat_axis=0, tiled=False)
 
@@ -378,15 +440,21 @@
 
     x_first = lanes(first_layer_input)
     cot = lanes(cotangent)
-    x_first_full = rows_of(x_first)
+    gain_pair = gains[0].T
+    gain_high, gain_rest = high_low(gain_pair)
+    gain_low = (gain_pair - gain_high.astype(F32) - gain_rest.astype(F32)).astype(BF16)
     w_qkv = qkv_weight[0]
-    w_qkv_group = exchange(
-        jnp.transpose(w_qkv.reshape(OWN, KV_HEADS, GROUP_COLS), (1, 0, 2)), "wa"
-    ).reshape(WIDTH, GROUP_COLS)
-    small = rows_of(jnp.concatenate([gains[0].T, router_weight[0].astype(F32)], axis=1))
-    gain_one, gain_two = small[:, 0:1], small[:, 1:2]
-    w_router = small[:, 2:].astype(BF16)
-    w_attn_full = rows_of(out_weight[0])
+    w_qkv_blocks = jnp.transpose(w_qkv.reshape(OWN, KV_HEADS, GROUP_COLS), (1, 0, 2))
+    packed = jnp.concatenate([x_first, router_weight[0], gain_high, gain_rest, gain_low], axis=1)
+    packed, w_qkv_blocks = lax.optimization_barrier((packed, w_qkv_blocks))
+    w_qkv_group = exchange(w_qkv_blocks, "wa").reshape(WIDTH, GROUP_COLS)
+    packed = rows_of(packed)
+    x_first_full = packed[:, :TOKENS]
+    w_router = packed[:, TOKENS : TOKENS + EXPERTS]
+    gain_parts = packed[:, TOKENS + EXPERTS :].astype(F32)
+    gain_parts = gain_parts[:, 0:2] + gain_parts[:, 2:4] + gain_parts[:, 4:6]
+    gain_one, gain_two = gain_parts[:, 0:1], gain_parts[:, 1:2]
+    w_attn_full = rows_of(after(out_weight[0], packed, w_qkv_group))
     w_attn_group = lax.dynamic_slice_in_dim(w_attn_full, w_index * OWN, OWN, 1)
     cot_full = rows_of(cot)
     w_in = expert_in[0]
@@ -411,8 +479,6 @@
     micro = jnp.arange(MICRO, dtype=jnp.int32).astype(F32)[:, None, None]
     place = lanes(jnp.where(chosen > 0.5, rank + CAP * micro, -1.0))
     chosen = lanes(chosen) > 0.5
-    places_all = lax.all_gather(place.astype(BF16), "seq", axis=0, tiled=False)
-    places_all = places_all.astype(F32)[:, :, None, :]
     places = place[:, None, :]
     route_lanes = jnp.concatenate([routes[0, 0].T, routes[0, 1].T], axis=1)
     picked = (
@@ -422,7 +488,19 @@
     def norm_scale(values):
         return lax.rsqrt(jnp.mean(values * values, axis=0, keepdims=True) + EPSILON)
 
-    def forward(x_own, x_full):
+    def for_seq(blocks, shared):
+        blocks = jnp.transpose(blocks.astype(BF16).reshape(OWN, N_SEQ, -1), (1, 0, 2))
+        shared = jnp.concatenate(high_low(shared), axis=1)
+        return jnp.concatenate(
+            [blocks, jnp.broadcast_to(shared[None], (N_SEQ,) + shared.shape)], axis=2
+        )
+
+    def from_seq(blocks, n):
+        total = jnp.sum(blocks.astype(F32), axis=0)
+        k = (total.shape[1] - n) // 2
+        return total[:, :n], total[:, n : n + k] + total[:, n + k :]
+
+    def forward(x_own, x_full, riders):
         x = x_full.astype(F32)
         scale_one = norm_scale(x)
         normed_one = (x * scale_one * gain_one).astype(BF16)
@@ -431,12 +509,10 @@
         turned = jnp.concatenate([turned, heads[PER_GROUP + 1 :]], axis=0).astype(BF16)
         turned = turned.reshape(GROUP_COLS, TOKENS)
         queries = turned[: PER_GROUP * HEAD_DIM]
-        key_value = exchange(
-            jnp.broadcast_to(
-                turned[PER_GROUP * HEAD_DIM :][None], (N_SEQ, 2 * HEAD_DIM, TOKENS)
-            ),
-            "seq",
-        )
+        sent = jnp.concatenate([turned[PER_GROUP * HEAD_DIM :]] + riders, axis=0)
+        key_value = exchange(jnp.broadcast_to(sent[None], (N_SEQ,) + sent.shape), "seq")
+        ridden = key_value[:, 2 * HEAD_DIM :]
+        key_value = key_value[:, : 2 * HEAD_DIM]
         mixed, log_total = attention_forward(first, queries, key_value)
         mixed_full = rows_of(mixed)
         middle = x + dot_nn(w_attn_full, mixed_full)
@@ -449,7 +525,7 @@
             0.0,
         )
         gates = raised / jnp.sum(raised, axis=0, keepdims=True)
-        part, g, u, compact = experts_forward(
+        part, compact, g, u = experts_forward(
             normed_two, gates[:, None, :], places, w_in, w_out
         )
         out = own(middle) + summed(part.reshape(N_WA, OWN, TOKENS), "wa")
@@ -470,9 +546,9 @@
             g,
             u,
         )
-        return out.astype(BF16), compact, saved
-
-    def backward(dz, dz_full, saved):
+        return out.astype(BF16), compact, saved, ridden
+
+    def backward(dz, dz_full, saved, alongside, later):
         (
             x_own,
             scale_one,
@@ -493,6 +569,10 @@
         part, dgate, du = experts_backward(
             dz_full, g, u, gates[:, None, :], places, w_in, w_out
         )
+        part, alongside = lax.optimization_barrier((part, alongside))
+        if later is not None:
+            du = of_section(du, later[0])
+            part, du = lax.optimization_barrier((part, du))
         inner = jnp.sum(part.astype(F32) * middle * gain_two, axis=0, keepdims=True)
         dgate_top = jnp.sum(jnp.where(picked, dgate[:, 0][None], 0.0), axis=1)
         extra = jnp.concatenate(
@@ -510,7 +590,11 @@
             ],
             axis=1,
         )
-        back = summed(blocks, "wa")
+        back = exchange(blocks, "wa")
+        if later is not None:
+            expert_out_grad = weight_grad_out(compact_out, alongside, places_all)
+            back, expert_out_grad = lax.optimization_barrier((back, expert_out_grad))
+        back = jnp.sum(back.astype(F32), axis=0)
         dgate_top = back[OWN : OWN + TOP]
         inner = back[OWN + TOP : OWN + TOP + 1] + back[OWN + TOP + 1 : OWN + TOP + 2]
         dgate = jnp.sum(jnp.where(picked, dgate_top[:, None, :], 0.0), axis=0)
@@ -530,7 +614,16 @@
         router_grad = dot_nt(own_normed_two, dlogit_high) + dot_nt(own_normed_two, dlogit_low)
         dmiddle_low = dmiddle.astype(BF16)
         attn_grad = dot_nt(dmiddle_low, mixed_full)
-        dmixed = dot_tn(w_attn_group, rows_of(dmiddle_low)).astype(BF16)
+        small_grad = jnp.concatenate([gain_two_grad, router_grad], axis=1)
+        if later is not None:
+            blocks = for_seq(of_section(attn_grad, later[1]), of_section(small_grad, later[2]))
+            dmiddle_low, blocks = lax.optimization_barrier((dmiddle_low, blocks))
+            attn_grad = exchange(blocks, "seq")
+        dmiddle_full = rows_of(dmiddle_low)
+        if later is not None:
+            dmiddle_full, attn_grad = lax.optimization_barrier((dmiddle_full, attn_grad))
+            attn_grad, small_grad = from_seq(attn_grad, OWN)
+        dmixed = dot_tn(w_attn_group, dmiddle_full).astype(BF16)
         dq, dkv = attention_backward(first, queries, key_value, mixed, dmixed, log_total)
         dkv = summed(dkv, "seq")
         dturned = jnp.concatenate([dq, dkv], axis=0)
@@ -542,19 +635,15 @@
         dheads = jnp.concatenate(
             [rotate(dheads[: PER_GROUP + 1], cosine, -sine), dheads[PER_GROUP + 1 :]], axis=0
         )
-        full = lax.all_gather(
-            jnp.concatenate(
-                [
-                    dheads.reshape(GROUP_COLS, TOKENS).astype(BF16),
-                    *high_low(inner_one),
-                    jnp.zeros((14, TOKENS), BF16),
-                ],
-                axis=0,
-            ),
-            "wa",
+        sent = jnp.concatenate(
+            [
+                dheads.reshape(GROUP_COLS, TOKENS).astype(BF16),
+                *high_low(inner_one),
+                jnp.zeros((14, TOKENS), BF16),
+            ],
             axis=0,
-            tiled=False,
-        )
+        )
+        full = exchange(jnp.broadcast_to(sent[None], (N_WA,) + sent.shape), "wa")
         dheads_full = full[:, :GROUP_COLS].reshape(KV_HEADS * GROUP_COLS, TOKENS)
         inner_one = jnp.sum(
             full[:, GROUP_COLS : GROUP_COLS + 2].astype(F32), axis=(0, 1)
@@ -568,49 +657,37 @@
         )
         gain_one_grad = jnp.sum(dnormed_one * x * scale_one, axis=1, keepdims=True)
         qkv_grad = dot_nt(own_normed_one, dheads_full)
-        return dx, du, gain_one_grad, gain_two_grad, router_grad, attn_grad, qkv_grad
-
-    out_one, compact_one, saved_one = forward(x_first, x_first_full)
+        if later is None:
+            return dx, alongside, (du, attn_grad, small_grad, gain_one_grad, qkv_grad)
+        blocks = for_seq(of_section(qkv_grad, later[4]), of_section(gain_one_grad, later[3]))
+        qkv_grad, gain_one_grad = from_seq(exchange(blocks, "seq"), GROUP_COLS)
+        return dx, expert_out_grad, (du, attn_grad, small_grad, gain_one_grad, qkv_grad)
+
+    riders = [jnp.concatenate([place, jnp.zeros((8, TOKENS), F32)], axis=0).astype(BF16)]
+    out_one, compact_one, saved_one, ridden = forward(x_first, x_first_full, riders)
+    places_all = ridden[:, :EXPERTS].astype(F32)[:, :, None, :]
     received = lax.ppermute(out_one, "section", [(0, 1)])
-    out_two, compact_two, saved_two = forward(received, rows_of(received))
+    out_two, compact_two, saved_two, _ = forward(received, rows_of(received), [])
 
     feature_in = exchange(
         of_section(saved_one[10], saved_two[10]).reshape(N_SEQ, OWN, TOKENS), "seq"
     )
     compact_out = lax.all_gather(of_section(compact_one, compact_two), "seq", axis=0, tiled=False)
 
-    back_two = backward(cot, cot_full, saved_two)
-    returned = lax.ppermute(back_two[0].astype(BF16), "section", [(1, 0)])
+    back_two = backward(cot, cot_full, saved_two, feature_in, None)
+    feature_in = back_two[1]
+    returned = lax.ppermute(
+        after(back_two[0].astype(BF16), compact_out), "section", [(1, 0)]
+    )
     returned_full = rows_of(returned)
     feature_out = exchange(
         of_section(returned_full, cot_full).reshape(N_SEQ, OWN, TOKENS), "seq"
     )
-    expert_out_grad = weight_grad(compact_out, feature_out, places_all)
-    back_one = backward(returned, returned_full, saved_one)
-
-    compact_in = lax.all_gather(of_section(back_one[1], back_two[1]), "seq", axis=0, tiled=False)
-    expert_in_grad = weight_grad(compact_in, feature_in, places_all)
-    gain_one_grad, gain_two_grad, router_grad, attn_grad, qkv_grad = (
-        of_section(one, two) for one, two in zip(back_one[2:], back_two[2:])
-    )
-    small_grad = lax.psum(jnp.concatenate([gain_two_grad, router_grad], axis=1), "seq")
-    attn_grad = summed(
-        jnp.transpose(attn_grad.astype(BF16).reshape(OWN, N_SEQ, OWN), (1, 0, 2)), "seq"
-    )
-    qkv_blocks = jnp.transpose(
-        qkv_grad.astype(BF16).reshape(OWN, N_SEQ, GROUP_COLS), (1, 0, 2)
-    )
-    gain_blocks = jnp.concatenate(
-        [*high_low(gain_one_grad), jnp.zeros((OWN, 384 - GROUP_COLS - 2), BF16)], axis=1
-    )
-    qkv_grad = summed(
-        jnp.concatenate(
-            [qkv_blocks, jnp.broadcast_to(gain_blocks[None], (N_SEQ,) + gain_blocks.shape)],
-            axis=2,
-        ),
-        "seq",
-    )
-    gain_one_grad = qkv_grad[:, GROUP_COLS] + qkv_grad[:, GROUP_COLS + 1]
+    back_one = backward(returned, returned_full, saved_one, feature_out, back_two[2])
+    expert_out_grad = back_one[1]
+    compact_in, attn_grad, small_grad, gain_one_grad, qkv_grad = back_one[2]
+    compact_in = lax.all_gather(compact_in, "seq", axis=0, tiled=False)
+    expert_in_grad = weight_grad_in(compact_in, feature_in, places_all)
 
     def tokens_first(values):
         return jnp.transpose(values.reshape(OWN, MICRO, ROWS), (1, 2, 0))[None]
@@ -618,8 +695,8 @@
     return (
         tokens_first(of_section(out_one, out_two)),
         tokens_first(of_section(back_one[0], back_two[0])),
-        jnp.stack([gain_one_grad, small_grad[:, 0]])[None],
-        qkv_grad[None, :, :GROUP_COLS],
+        jnp.stack([gain_one_grad[:, 0], small_grad[:, 0]])[None],
+        qkv_grad[None],
         attn_grad[None],
         small_grad[None, :, 1:],
         expert_in_grad.reshape(1, EXPERTS, 2, HIDDEN, OWN),

time: 670 us -> 542 us (0.81)
  blocking collectives: 227 us -> 150 us
  Pallas kernels: 127 us -> 86.4 us
  waiting for transfers between devices: 123 us -> 104 us
  local copies, waits for them, and re-layouts: 31.7 us -> 40.2 us
    all_gather x3 -> x1, waiting for transfers between devices: 48.8 us -> 0.01 us  [on_device(): compact_in = lax.all_gather(compact_in, 'seq', axis=0, tiled=False)]
    psum x1 -> x0, blocking collectives: 35.5 us -> none  [on_device(): lax.psum(jnp.concatenate([gain_two_grad, router_grad], axis=1), 'seq')]
    pallas_call x6, Pallas kernels: 107 us -> 71.5 us  [the longest x2 29.1 us: experts_backward(): pl.pallas_call(experts_backward_kernel, in_specs=[vmem_spec(), vmem_spec(...]
    all_to_all x12 -> x14, waiting for transfers between devices: 67.6 us -> 100 us  [exchange(): lax.all_to_all(blocks, axis, split_axis=0, concat_axis=0, tiled=False)]
    all_gather x1 -> x0, blocking collectives: 28.3 us -> none  [on_device(): places_all = lax.all_gather(place.astype(BF16), 'seq', axis=0, tiled=False)]
    all_gather x9 -> x8, blocking collectives: 148 us -> 127 us  [rows_of(): return lax.all_gather(values, 'wa', axis=0, tiled=True)]
    unnamed x235 -> x244, local copies, waits for them, and re-layouts: 6.09 us -> 23.7 us
    all_to_all x12 -> x14, starting transfers between devices: 65.5 us -> 72.8 us  [exchange(): lax.all_to_all(blocks, axis, split_axis=0, concat_axis=0, tiled=False)]
  transfers between devices with their start and end apart: 19 -> 19, of which waited for: 11 -> 11; matrix products, arithmetic and copies ran while one was open for 8% -> 10% of each run, Pallas kernels for 3% -> 12%
where the time goes in v2:
time: 542 us; the launch traced here: 534 us
  blocking collectives  150 us (28%)
  waiting for transfers between devices  104 us (19%)
  Pallas kernels  86.4 us (16%)
  starting transfers between devices  76.8 us (14%)
  local copies, waits for them, and re-layouts  40.2 us (7%)
  other arithmetic  30.5 us (6%)
  matrix products  30.1 us (6%)
  between operations  15.9 us (3%)
    all_gather x8, blocking collectives, rows_of(): return lax.all_gather(values, 'wa', axis=0, tiled=True)  127 us
    all_to_all x14, waiting for transfers between devices, exchange(): lax.all_to_all(blocks, axis, split_axis=0, concat_axis=0, tiled=False)  100 us
    all_to_all x14, starting transfers between devices, exchange(): lax.all_to_all(blocks, axis, split_axis=0, concat_axis=0, tiled=False)  72.8 us
    pallas_call x2, Pallas kernels, experts_backward(): pl.pallas_call(experts_backward_kernel, in_specs=[vmem_spec(), vmem_spec(...  29.1 us
    pallas_call x2, Pallas kernels, experts_forward(): pl.pallas_call(experts_forward_kernel, in_specs=[vmem_spec(), vmem_spec()...  24.1 us
    unnamed x244, local copies, waits for them, and re-layouts  23.7 us
    all_to_all x1, blocking collectives, exchange(): lax.all_to_all(blocks, axis, split_axis=0, concat_axis=0, tiled=False)  23.1 us
    pallas_call x2, Pallas kernels, weight_grad(): pl.pallas_call(kernel, grid=(EXPERTS // QUAD,), in_specs=[pl.BlockSpec((N...  18.3 us
  transfers between devices with their start and end apart: 19, of which 11 were waited for; matrix products, arithmetic and copies ran while one was open for 10% of the time, Pallas kernels for 12%

profile of v2, /device:TPU:1, one launch (start us, length us, event | category | flops | bytes accessed | tf_op | source)
XLA Modules:
  0.0 534.1 jit_solution(8139168092789203669)
XLA Ops:
  9.7 2.0 reshape_squeeze.3
  13.1 5.8 %all-to-all-start = ((bf16[8,192,320]{2,1,0:T(8,128)(2,1)}), bf16[8,192,320]{2,1,0:T(8,128)(2,1)S(1)}, u32[]{:S(2)}, u32[]{:S(2)}) async-start(bf16[8,192,320]{2,1,0:T(8,128)(2,1)} %bitcast.222), calls=%async_computation | async-start | bytes 2359296 | tf_op jit(solution)/shard_map/all_to_all | solution.py:406
  18.9 26.5 %all_gather.39 = bf16[1536,302]{1,0:T(8,128)(2,1)S(1)} all-gather(bf16[192,302]{1,0:T(8,128)(2,1)S(1)} %concatenate.105), channel_id=1, replica_groups=mesh['section'=2,'seq'=8,'wa'=8] {'wa'}, dimensions={0}, use_global_device_ids=true | all-gather | bytes 1043712 | tf_op jit(solution)/shard_map/all_gather | solution.py:430
  50.6 7.5 %all-to-all-start.1 = ((bf16[8,176,256]{2,1,0:T(8,128)(2,1)}), bf16[8,176,256]{2,1,0:T(8,128)(2,1)S(1)}, u32[]{:S(2)}, u32[]{:S(2)}) async-start(bf16[8,176,256]{2,1,0:T(8,128)(2,1)} %broadcast_in_dim.187), calls=%async_computation.1 | async-start | bytes 1441792 | tf_op jit(solution)/shard_map/all_to_all | solution.py:406
  58.8 11.7 %all-to-all-done.1 = bf16[8,176,256]{2,1,0:T(8,128)(2,1)S(1)} async-done(((bf16[8,176,256]{2,1,0:T(8,128)(2,1)}), bf16[8,176,256]{2,1,0:T(8,128)(2,1)S(1)}, u32[]{:S(2)}, u32[]{:S(2)}) %all-to-all-start.1) | async-done | bytes 720928 | tf_op jit(solution)/shard_map/all_to_all | solution.py:406
  70.5 3.7 attention_forward.2
  75.0 14.5 %all_gather.41 = bf16[1536,256]{1,0:T(8,128)(2,1)S(1)} all-gather(bf16[192,256]{1,0:T(8,128)(2,1)S(1)} %get-tuple-element.49.o_ref), channel_id=1, replica_groups=mesh['section'=2,'seq'=8,'wa'=8] {'wa'}, dimensions={0}, use_global_device_ids=true | all-gather | bytes 884736 | tf_op jit(solution)/shard_map/all_gather | solution.py:430
  89.5 4.2 multiply_reduce_fusion.3
  96.6 12.0 %experts_forward.2 = (bf16[1536,256]{1,0:T(8,128)(2,1)}, bf16[1280,128]{1,0:T(8,128)(2,1)S(1)}, bf16[2560,256]{1,0:T(8,128)(2,1)S(1)}, bf16[2560,256]{1,0:T(8,128)(2,1)S(1)}) custom-call(bf16[1536,256]{1,0:T(8,128)(2,1)S(1)} %multiply_convert_fusion.1.x_ref, f32[40,1,256]{2,1,0:T(1,128)S(1)} %copy.122.gate_ref, ...), custom_call_target="tpu_custom_call" | custom-call | flops 6039797760 | bytes 28000000 | tf_op jit(solution)/shard_map/experts_forward/pallas_call | solution.py:154
  111.5 3.7 all-to-all-start.2
  116.8 10.8 %all-to-all-done.2 = bf16[8,192,256]{2,1,0:T(8,128)(2,1)S(1)} async-done(((bf16[8,192,256]{2,1,0:T(8,128)(2,1)}), bf16[8,192,256]{2,1,0:T(8,128)(2,1)S(1)}, u32[]{:S(2)}, u32[]{:S(2)}) %all-to-all-start.2) | async-done | bytes 786464 | tf_op jit(solution)/shard_map/all_to_all | solution.py:406
  127.7 2.7 collective-permute-start
  130.4 1.6 collective-permute-done
  132.0 15.0 %all_gather.42 = bf16[1536,256]{1,0:T(8,128)(2,1)S(1)} all-gather(bf16[192,256]{1,0:T(8,128)(2,1)S(1)} %collective-permute-done), channel_id=1, replica_groups=mesh['section'=2,'seq'=8,'wa'=8] {'wa'}, dimensions={0}, use_global_device_ids=true | all-gather | bytes 884736 | tf_op jit(solution)/shard_map/all_gather | solution.py:430
  150.6 4.9 all-to-all-start.3
  155.6 14.0 %all_gather.44.dz_ref = bf16[1536,256]{1,0:T(8,128)(2,1)S(1)} all-gather(bf16[192,256]{1,0:T(8,128)(2,1)S(1)} %copy-done.71), channel_id=1, replica_groups=mesh['section'=2,'seq'=8,'wa'=8] {'wa'}, dimensions={0}, use_global_device_ids=true | all-gather | bytes 884736 | tf_op jit(solution)/shard_map/all_gather | solution.py:430
  169.6 3.7 attention_forward.3
  173.2 13.5 %all_gather.43 = bf16[1536,256]{1,0:T(8,128)(2,1)S(1)} all-gather(bf16[192,256]{1,0:T(8,128)(2,1)S(1)} %get-tuple-element.51.o_ref), channel_id=1, replica_groups=mesh['section'=2,'seq'=8,'wa'=8] {'wa'}, dimensions={0}, use_global_device_ids=true | all-gather | bytes 884736 | tf_op jit(solution)/shard_map/all_gather | solution.py:430
  186.7 4.3 multiply_reduce_fusion.2
  191.1 1.4 broadcast_select_fusion.1
  193.9 6.9 %all-to-all-start.5 = ((bf16[8,192,256]{2,1,0:T(8,128)(2,1)}), bf16[8,192,256]{2,1,0:T(8,128)(2,1)}, u32[]{:S(2)}, u32[]{:S(2)}) async-start(bf16[8,192,256]{2,1,0:T(8,128)(2,1)} %bitcast.251), calls=%async_computation.5 | async-start | bytes 1572864 | tf_op jit(solution)/shard_map/all_to_all | solution.py:406
  200.8 12.1 %experts_forward.3 = (bf16[1536,256]{1,0:T(8,128)(2,1)}, bf16[1280,128]{1,0:T(8,128)(2,1)S(1)}, bf16[2560,256]{1,0:T(8,128)(2,1)S(1)}, bf16[2560,256]{1,0:T(8,128)(2,1)S(1)}) custom-call(bf16[1536,256]{1,0:T(8,128)(2,1)S(1)} %get-tuple-element.117.x_ref, f32[40,1,256]{2,1,0:T(1,128)S(1)} %copy.123.gate_ref, f32[40,1,256]{2,1,0:T(1,128)S(1)} %broadcast_in_dim.191.place_ref, ...), custom_call_target="tpu_custom_call" | custom-call | flops 6039797760 | bytes 28000000 | tf_op jit(solution)/shard_map/experts_forward/pallas_call | solution.py:154
  213.6 14.5 %experts_backward.2 = (bf16[1536,256]{1,0:T(8,128)(2,1)S(1)}, f32[40,1,256]{2,1,0:T(1,128)S(1)}, bf16[2560,128]{1,0:T(8,128)(2,1)S(1)}) custom-call(bf16[1536,256]{1,0:T(8,128)(2,1)S(1)} %all_gather.44.dz_ref, f32[40,1,256]{2,1,0:T(1,128)S(1)} %copy.123.gate_ref, f32[40,1,256]{2,1,0:T(1,128)S(1)} %broadcast_in_dim.191.place_ref, ...), custom_call_target="tpu_custom_call" | custom-call | flops 6039797760 | bytes 28000000 | tf_op jit(solution)/shard_map/experts_backward/pallas_call | solution.py:219
  229.9 2.0 multiply_reduce_fusion.1
  233.0 4.5 all-to-all-start.6
  238.1 1.8 broadcast_select_fusion.3
  239.9 10.8 %all-to-all-done.6 = bf16[8,208,256]{2,1,0:T(8,128)(2,1)} async-done(((bf16[8,208,256]{2,1,0:T(8,128)(2,1)}), bf16[8,208,256]{2,1,0:T(8,128)(2,1)}, u32[]{:S(2)}, u32[]{:S(2)}) %all-to-all-start.6) | async-done | bytes 852000 | tf_op jit(solution)/shard_map/all_to_all | solution.py:406
  253.1 2.5 fusion.101
  256.2 14.2 %all_gather.45 = bf16[1536,256]{1,0:T(8,128)(2,1)S(1)} all-gather(bf16[192,256]{1,0:T(8,128)(2,1)S(1)} %get-tuple-element.112), channel_id=1, replica_groups=mesh['section'=2,'seq'=8,'wa'=8] {'wa'}, dimensions={0}, use_global_device_ids=true | all-gather | bytes 884736 | tf_op jit(solution)/shard_map/all_gather | solution.py:430
  270.4 1.9 convolution_convert_fusion.1.do_ref
  272.4 3.6 attention_backward.2
  276.8 7.1 %all-to-all-start.7 = ((bf16[8,128,256]{2,1,0:T(8,128)(2,1)}), bf16[8,128,256]{2,1,0:T(8,128)(2,1)}, u32[]{:S(2)}, u32[]{:S(2)}) async-start(bf16[8,128,256]{2,1,0:T(8,128)(2,1)} %copy-done.12), calls=%async_computation.7 | async-start | bytes 1048576 | tf_op jit(solution)/shard_map/all_to_all | solution.py:406
  285.3 9.5 %all-to-all-done.7 = bf16[8,128,256]{2,1,0:T(8,128)(2,1)} async-done(((bf16[8,128,256]{2,1,0:T(8,128)(2,1)}), bf16[8,128,256]{2,1,0:T(8,128)(2,1)}, u32[]{:S(2)}, u32[]{:S(2)}) %all-to-all-start.7) | async-done | bytes 524320 | tf_op jit(solution)/shard_map/all_to_all | solution.py:406
  297.3 23.1 %all_to_all.75 = bf16[8,336,256]{2,1,0:T(8,128)(2,1)S(1)} all-to-all(bf16[8,336,256]{2,1,0:T(8,128)(2,1)S(1)} %broadcast_in_dim.201), channel_id=1, replica_groups=mesh['section'=2,'seq'=8,'wa'=8] {'wa'}, dimensions={0} | all-to-all | bytes 2752512 | tf_op jit(solution)/shard_map/all_to_all | solution.py:406
  326.4 2.2 collective-permute-done.1
  328.6 15.2 %all_gather.48.dz_ref = bf16[1536,256]{1,0:T(8,128)(2,1)S(1)} all-gather(bf16[192,256]{1,0:T(8,128)(2,1)S(1)} %collective-permute-done.1), channel_id=1, replica_groups=mesh['section'=2,'seq'=8,'wa'=8] {'wa'}, dimensions={0}, use_global_device_ids=true | all-gather | bytes 884736 | tf_op jit(solution)/shard_map/all_gather | solution.py:430
  344.8 4.2 all-to-all-start.9
  350.3 1.3 copy-done.8
  351.6 14.6 %experts_backward.3 = (bf16[1536,256]{1,0:T(8,128)(2,1)S(1)}, f32[40,1,256]{2,1,0:T(1,128)S(1)}, bf16[2560,128]{1,0:T(8,128)(2,1)S(1)}) custom-call(bf16[1536,256]{1,0:T(8,128)(2,1)S(1)} %all_gather.48.dz_ref, f32[40,1,256]{2,1,0:T(1,128)S(1)} %copy.122.gate_ref, f32[40,1,256]{2,1,0:T(1,128)S(1)} %broadcast_in_dim.191.place_ref, ...), custom_call_target="tpu_custom_call" | custom-call | flops 6039797760 | bytes 28000000 | tf_op jit(solution)/shard_map/experts_backward/pallas_call | solution.py:219
  367.3 1.7 multiply_reduce_fusion
  370.1 3.6 all-to-all-start.10
  374.1 2.4 fusion.106
  376.5 1.7 copy-done.19
  378.2 9.0 %expert_weight_grad.2 = f32[40,64,192]{2,1,0:T(8,128)} custom-call(bf16[8,1280,128]{2,1,0:T(8,128)(2,1)S(1)} %bitcast.236, bf16[8,192,256]{2,1,0:T(8,128)(2,1)} %all-to-all-done.9.feature_ref, f32[8,40,1,256]{3,2,1,0:T(1,128)S(1)} %copy-done.9), custom_call_target="tpu_custom_call" | custom-call | flops 2013265920 | bytes 15000000 | tf_op jit(solution)/shard_map/expert_weight_grad/pallas_call | solution.py:266
  388.0 1.9 multiply_reduce_fusion.5
  392.3 6.8 %all-to-all-start.11 = ((bf16[8,192,274]{1,2,0:T(8,128)(2,1)}), bf16[8,192,274]{1,2,0:T(8,128)(2,1)S(1)}, u32[]{:S(2)}, u32[]{:S(2)}) async-start(bf16[8,192,274]{1,2,0:T(8,128)(2,1)} %pad_maximum_fusion.1), calls=%async_computation.11 | async-start | bytes 2293760 | tf_op jit(solution)/shard_map/all_to_all | solution.py:406
  399.1 14.5 %all_gather.49 = bf16[1536,256]{1,0:T(8,128)(2,1)S(1)} all-gather(bf16[192,256]{1,0:T(8,128)(2,1)S(1)} %get-tuple-element.74), channel_id=1, replica_groups=mesh['section'=2,'seq'=8,'wa'=8] {'wa'}, dimensions={0}, use_global_device_ids=true | all-gather | bytes 884736 | tf_op jit(solution)/shard_map/all_gather | solution.py:430
  413.6 5.7 %all-to-all-done.11 = bf16[8,192,274]{1,2,0:T(8,128)(2,1)S(1)} async-done(((bf16[8,192,274]{1,2,0:T(8,128)(2,1)}), bf16[8,192,274]{1,2,0:T(8,128)(2,1)S(1)}, u32[]{:S(2)}, u32[]{:S(2)}) %all-to-all-start.11) | async-done | bytes 841760 | tf_op jit(solution)/shard_map/all_to_all | solution.py:406
  419.3 2.5 convolution_convert_fusion.do_ref
  421.8 4.0 attention_backward.3
  425.8 4.2 all-to-all-start.12
  430.0 11.4 %all-to-all-done.12 = bf16[8,128,256]{2,1,0:T(8,128)(2,1)S(1)} async-done(((bf16[8,128,256]{2,1,0:T(8,128)(2,1)}), bf16[8,128,256]{2,1,0:T(8,128)(2,1)S(1)}, u32[]{:S(2)}, u32[]{:S(2)}) %all-to-all-start.12) | async-done | bytes 524320 | tf_op jit(solution)/shard_map/all_to_all | solution.py:406
  442.3 5.4 %all-to-all-start.4 = ((bf16[8,192,256]{2,1,0:T(8,128)(2,1)}), bf16[8,192,256]{2,1,0:T(8,128)(2,1)S(1)}, u32[]{:S(2)}, u32[]{:S(2)}) async-start(bf16[8,192,256]{2,1,0:T(8,128)(2,1)} %bitcast.37), calls=%async_computation.4 | async-start | bytes 1572864 | tf_op jit(solution)/shard_map/all_to_all | solution.py:406
  449.2 10.8 %all-to-all-done.4 = bf16[8,192,256]{2,1,0:T(8,128)(2,1)S(1)} async-done(((bf16[8,192,256]{2,1,0:T(8,128)(2,1)}), bf16[8,192,256]{2,1,0:T(8,128)(2,1)S(1)}, u32[]{:S(2)}, u32[]{:S(2)}) %all-to-all-start.4) | async-done | bytes 786464 | tf_op jit(solution)/shard_map/all_to_all | solution.py:406
  461.2 4.3 all-to-all-start.13
  466.3 17.8 %all-to-all-done.13 = bf16[8,336,256]{2,1,0:T(8,128)(2,1)S(1)} async-done(((bf16[8,336,256]{2,1,0:T(8,128)(2,1)}), bf16[8,336,256]{2,1,0:T(8,128)(2,1)S(1)}, u32[]{:S(2)}, u32[]{:S(2)}) %all-to-all-start.13) | async-done | bytes 1376288 | tf_op jit(solution)/shard_map/all_to_all | solution.py:406
  487.4 2.1 fusion.40
  489.5 1.5 fusion
  493.4 3.7 all-to-all-start.14
  497.1 1.6 bitcast_bitcast_fusion.1
  498.7 1.5 convert_reduce_fusion.1
  502.4 11.6 %all-to-all-done.14 = bf16[8,192,322]{2,1,0:T(8,128)(2,1)S(1)} async-done(((bf16[8,192,322]{2,1,0:T(8,128)(2,1)}), bf16[8,192,322]{2,1,0:T(8,128)(2,1)S(1)}, u32[]{:S(2)}, u32[]{:S(2)}) %all-to-all-start.14) | async-done | bytes 989216 | tf_op jit(solution)/shard_map/all_to_all | solution.py:406
  515.6 2.5 copy-done
  518.1 9.3 %expert_weight_grad.3 = f32[40,128,192]{2,1,0:T(8,128)} custom-call(bf16[8,2560,128]{2,1,0:T(8,128)(2,1)S(1)} %bitcast.227, bf16[8,192,256]{2,1,0:T(8,128)(2,1)} %all-to-all-done.5.feature_ref, f32[8,40,1,256]{3,2,1,0:T(1,128)S(1)} %copy-done.9), custom_call_target="tpu_custom_call" | custom-call | flops 2013265920 | bytes 15000000 | tf_op jit(solution)/shard_map/expert_weight_grad/pallas_call | solution.py:266
  (420 shorter events, 61.5 us)
Async XLA Ops:
  13.1 32.4 %copy-start.87 = (s32[1,2,128,8]{2,3,1,0:T(8,128)S(1)}, s32[1,2,128,8]{2,3,1,0:T(8,128)}, u32[]{:S(2)}) copy-start(s32[1,2,128,8]{2,3,1,0:T(8,128)} %param.10) | copy-start | bytes 24580
  13.1 32.3 %all-to-all-start = ((bf16[8,192,320]{2,1,0:T(8,128)(2,1)}), bf16[8,192,320]{2,1,0:T(8,128)(2,1)S(1)}, u32[]{:S(2)}, u32[]{:S(2)}) async-start(bf16[8,192,320]{2,1,0:T(8,128)(2,1)} %bitcast.222), calls=%async_computation | async-start | bytes 2359296 | tf_op jit(solution)/shard_map/all_to_all | solution.py:406
  18.9 70.7 %all-gather.6.cloned.1.call-start = ((), (), s32[]{:S(2)}) async-start(), calls=%async_computation.15 | async-start | bytes 5308416 | tf_op jit(solution)/shard_map/all_gather | solution.py:430
  47.0 182.9 %copy-start.77 = (f32[1536]{0:T(1024)}, f32[1536]{0:T(1024)S(1)}, u32[]{:S(2)}) copy-start(f32[1536]{0:T(1024)S(1)} %get-tuple-element.108) | copy-start | bytes 18436
  47.8 101.9 %copy-start.56 = (f32[32,256]{1,0:T(8,128)}, f32[32,256]{1,0:T(8,128)S(1)}, u32[]{:S(2)}) copy-start(f32[32,256]{1,0:T(8,128)S(1)} %get-tuple-element.170) | copy-start | bytes 98308
  50.6 19.9 %all-to-all-start.1 = ((bf16[8,176,256]{2,1,0:T(8,128)(2,1)}), bf16[8,176,256]{2,1,0:T(8,128)(2,1)S(1)}, u32[]{:S(2)}, u32[]{:S(2)}) async-start(bf16[8,176,256]{2,1,0:T(8,128)(2,1)} %broadcast_in_dim.187), calls=%async_computation.1 | async-start | bytes 1441792 | tf_op jit(solution)/shard_map/all_to_all | solution.py:406
  70.5 19.1 %copy-start.34 = (bf16[8,176,256]{2,1,0:T(8,128)(2,1)}, bf16[8,176,256]{2,1,0:T(8,128)(2,1)S(1)}, u32[]{:S(2)}) copy-start(bf16[8,176,256]{2,1,0:T(8,128)(2,1)S(1)} %all-to-all-done.1) | copy-start | bytes 2162692
  75.0 18.8 %copy-start.15 = (f32[3,1,256]{2,1,0:T(1,128)}, f32[3,1,256]{2,1,0:T(1,128)S(1)}, u32[]{:S(2)}) copy-start(f32[3,1,256]{2,1,0:T(1,128)S(1)} %get-tuple-element.77.lse_ref) | copy-start | bytes 9220
  93.8 33.9 %copy-start.20 = (f32[1536,256]{1,0:T(8,128)}, f32[1536,256]{1,0:T(8,128)S(1)}, u32[]{:S(2)}) copy-start(f32[1536,256]{1,0:T(8,128)S(1)} %get-tuple-element.158) | copy-start | bytes 4718596
  95.9 12.7 %copy-start.89 = (f32[256]{0:T(256)}, f32[256]{0:T(256)S(1)}, u32[]{:S(2)}) copy-start(f32[256]{0:T(256)S(1)} %get-tuple-element.118) | copy-start | bytes 3076
  95.9 156.1 %copy-start.41 = (pred[40,256]{1,0:T(8,128)(4,1)}, pred[40,256]{1,0:T(8,128)(4,1)S(1)}, u32[]{:S(2)}) copy-start(pred[40,256]{1,0:T(8,128)(4,1)S(1)} %get-tuple-element.119) | copy-start | bytes 30724
  96.5 12.1 %copy-start.91 = (f32[256]{0:T(256)}, f32[256]{0:T(256)S(1)}, u32[]{:S(2)}) copy-start(f32[256]{0:T(256)S(1)} %fusion.58) | copy-start | bytes 3076
  111.5 5.3 copy-start.88
  111.5 16.1 %all-to-all-start.2 = ((bf16[8,192,256]{2,1,0:T(8,128)(2,1)}), bf16[8,192,256]{2,1,0:T(8,128)(2,1)S(1)}, u32[]{:S(2)}, u32[]{:S(2)}) async-start(bf16[8,192,256]{2,1,0:T(8,128)(2,1)} %bitcast.31), calls=%async_computation.2 | async-start | bytes 1572864 | tf_op jit(solution)/shard_map/all_to_all | solution.py:406
  116.8 31.7 %copy-start.83 = (f32[1536]{0:T(1024)S(1)}, f32[1536]{0:T(1024)}, u32[]{:S(2)}) copy-start(f32[1536]{0:T(1024)} %copy-done.82) | copy-start | bytes 18436
  127.7 21.1 %copy-start.69 = (bf16[192,256]{1,0:T(8,128)(2,1)}, bf16[192,256]{1,0:T(8,128)(2,1)S(1)}, u32[]{:S(2)}) copy-start(bf16[192,256]{1,0:T(8,128)(2,1)S(1)} %add_convert_fusion.1) | copy-start | bytes 294916
  127.7 4.3 collective-permute-start
  130.4 121.6 %copy-start.79 = (s32[8,256]{1,0:T(8,128)}, s32[8,256]{1,0:T(8,128)S(1)}, u32[]{:S(2)}) copy-start(s32[8,256]{1,0:T(8,128)S(1)} %pad_add_fusion) | copy-start | bytes 24580
  130.4 18.4 %copy-start.40 = (bf16[8,192,320]{2,1,0:T(8,128)(2,1)S(1)}, bf16[8,192,320]{2,1,0:T(8,128)(2,1)}, u32[]{:S(2)}) copy-start(bf16[8,192,320]{2,1,0:T(8,128)(2,1)} %copy-done.39) | copy-start | bytes 2949124
  132.0 15.3 %copy-start.49 = (bf16[192,256]{1,0:T(8,128)(2,1)}, bf16[192,256]{1,0:T(8,128)(2,1)S(1)}, u32[]{:S(2)}) copy-start(bf16[192,256]{1,0:T(8,128)(2,1)S(1)} %collective-permute-done) | copy-start | bytes 294916
  149.7 5.9 %copy-start.71 = (bf16[192,256]{1,0:T(8,128)(2,1)S(1)}, bf16[192,256]{1,0:T(8,128)(2,1)}, u32[]{:S(2)}) copy-start(bf16[192,256]{1,0:T(8,128)(2,1)} %pad_maximum_fusion.10) | copy-start | bytes 294916
  150.6 18.9 %all-to-all-start.3 = ((bf16[8,128,256]{2,1,0:T(8,128)(2,1)}), bf16[8,128,256]{2,1,0:T(8,128)(2,1)S(1)}, u32[]{:S(2)}, u32[]{:S(2)}) async-start(bf16[8,128,256]{2,1,0:T(8,128)(2,1)} %broadcast_in_dim.193), calls=%async_computation.3 | async-start | bytes 1048576 | tf_op jit(solution)/shard_map/all_to_all | solution.py:406
  155.6 76.3 %copy-start.118 = (bf16[16]{0:T(256)(128)(2,1)}, bf16[16]{0:T(256)(128)(2,1)S(1)}, u32[]{:S(2)}) copy-start(bf16[16]{0:T(256)(128)(2,1)S(1)} %pad.51.clone) | copy-start | bytes 100
  173.2 17.8 %copy-start.17 = (f32[3,1,256]{2,1,0:T(1,128)}, f32[3,1,256]{2,1,0:T(1,128)S(1)}, u32[]{:S(2)}) copy-start(f32[3,1,256]{2,1,0:T(1,128)S(1)} %get-tuple-element.58.lse_ref) | copy-start | bytes 9220
  193.9 36.0 %all-to-all-start.5 = ((bf16[8,192,256]{2,1,0:T(8,128)(2,1)}), bf16[8,192,256]{2,1,0:T(8,128)(2,1)}, u32[]{:S(2)}, u32[]{:S(2)}) async-start(bf16[8,192,256]{2,1,0:T(8,128)(2,1)} %bitcast.251), calls=%async_computation.5 | async-start | bytes 1572864 | tf_op jit(solution)/shard_map/all_to_all | solution.py:406
  232.0 5.5 %copy-start.114 = (f32[1,2,192]{2,1,0:T(2,128)S(1)}, f32[1,2,192]{2,1,0:T(2,128)}, u32[]{:S(2)}) copy-start(f32[1,2,192]{2,1,0:T(2,128)} %param.12) | copy-start | bytes 4612
  233.0 17.6 %all-to-all-start.6 = ((bf16[8,208,256]{2,1,0:T(8,128)(2,1)}), bf16[8,208,256]{2,1,0:T(8,128)(2,1)}, u32[]{:S(2)}, u32[]{:S(2)}) async-start(bf16[8,208,256]{2,1,0:T(8,128)(2,1)} %pad_maximum_fusion.2), calls=%async_computation.6 | async-start | bytes 1703936 | tf_op jit(solution)/shard_map/all_to_all | solution.py:406
  237.5 15.3 %copy-start.66 = (bf16[1,192,40]{1,2,0:T(8,128)(2,1)S(1)}, bf16[1,192,40]{1,2,0:T(8,128)(2,1)}, u32[]{:S(2)}) copy-start(bf16[1,192,40]{1,2,0:T(8,128)(2,1)} %param.15) | copy-start | bytes 46084
  237.5 85.7 %all-gather.8.cloned.1.call-start = ((), (), s32[]{:S(2)}) async-start(), calls=%async_computation.16 | async-start | bytes 2949120 | tf_op jit(solution)/shard_map/all_gather | solution.py:675
  238.1 15.0 %copy-start.93 = (f32[1,1,192]{2,1,0:T(1,128)}, f32[1,1,192]{2,1,0:T(1,128)S(1)}, u32[]{:S(2)}) copy-start(f32[1,1,192]{2,1,0:T(1,128)S(1)} %get-tuple-element.154) | copy-start | bytes 2308
  252.1 20.3 %copy-start.43 = (f32[40,256]{1,0:T(8,128)}, f32[40,256]{1,0:T(8,128)S(1)}, u32[]{:S(2)}) copy-start(f32[40,256]{1,0:T(8,128)S(1)} %get-tuple-element.115) | copy-start | bytes 122884
  255.6 16.8 %copy-start.18 = (f32[3,1,256]{2,1,0:T(1,128)S(1)}, f32[3,1,256]{2,1,0:T(1,128)}, u32[]{:S(2)}) copy-start(f32[3,1,256]{2,1,0:T(1,128)} %copy-done.17) | copy-start | bytes 9220
  276.8 20.2 %copy-start.57 = (f32[32,256]{1,0:T(8,128)S(1)}, f32[32,256]{1,0:T(8,128)}, u32[]{:S(2)}) copy-start(f32[32,256]{1,0:T(8,128)} %copy-done.56) | copy-start | bytes 98308
  276.8 18.1 %all-to-all-start.7 = ((bf16[8,128,256]{2,1,0:T(8,128)(2,1)}), bf16[8,128,256]{2,1,0:T(8,128)(2,1)}, u32[]{:S(2)}, u32[]{:S(2)}) async-start(bf16[8,128,256]{2,1,0:T(8,128)(2,1)} %copy-done.12), calls=%async_computation.7 | async-start | bytes 1048576 | tf_op jit(solution)/shard_map/all_to_all | solution.py:406
  283.9 13.3 %copy-start.102 = (bf16[336]{0:T(512)(128)(2,1)}, bf16[336]{0:T(512)(128)(2,1)S(1)}, u32[]{:S(2)}) copy-start(bf16[336]{0:T(512)(128)(2,1)S(1)} %pad.38.clone) | copy-start | bytes 2020
  284.7 12.6 %copy-start.72 = (f32[32,256]{1,0:T(8,128)}, f32[32,256]{1,0:T(8,128)S(1)}, u32[]{:S(2)}) copy-start(f32[32,256]{1,0:T(8,128)S(1)} %fusion.95) | copy-start | bytes 98308
  323.2 5.3 %collective-permute-start.1 = (bf16[192,256]{1,0:T(8,128)(2,1)S(1)}, bf16[192,256]{1,0:T(8,128)(2,1)S(1)}, u32[]{:S(2)}, u32[]{:S(2)}) collective-permute-start(bf16[192,256]{1,0:T(8,128)(2,1)S(1)} %get-tuple-element.63), channel_id=1, source_target_pairs={{64,0},{65,1},{66,2},{67,3},{68,4},{69,5},{70,6},{71,7},{72,8},{73... | collective-permute-start | bytes 294920 | tf_op jit(solution)/shard_map/ppermute | solution.py:679
  328.6 59.4 %copy-start.52 = (bf16[192,256]{1,0:T(8,128)(2,1)}, bf16[192,256]{1,0:T(8,128)(2,1)S(1)}, u32[]{:S(2)}) copy-start(bf16[192,256]{1,0:T(8,128)(2,1)S(1)} %collective-permute-done.1) | copy-start | bytes 294916
  344.8 22.5 %all-to-all-start.9 = ((bf16[8,192,256]{2,1,0:T(8,128)(2,1)}), bf16[8,192,256]{2,1,0:T(8,128)(2,1)}, u32[]{:S(2)}, u32[]{:S(2)}) async-start(bf16[8,192,256]{2,1,0:T(8,128)(2,1)} %bitcast.252), calls=%async_computation.9 | async-start | bytes 1572864 | tf_op jit(solution)/shard_map/all_to_all | solution.py:406
  351.6 14.6 %copy-start.80 = (s32[8,256]{1,0:T(8,128)S(1)}, s32[8,256]{1,0:T(8,128)}, u32[]{:S(2)}) copy-start(s32[8,256]{1,0:T(8,128)} %copy-done.79) | copy-start | bytes 24580
  351.6 14.7 %copy-start.11 = (bf16[2560,128]{1,0:T(8,128)(2,1)S(1)}, bf16[2560,128]{1,0:T(8,128)(2,1)}, u32[]{:S(2)}) copy-start(bf16[2560,128]{1,0:T(8,128)(2,1)} %copy-done.10) | copy-start | bytes 1966084
  370.1 17.2 %all-to-all-start.10 = ((bf16[8,208,256]{2,1,0:T(8,128)(2,1)}), bf16[8,208,256]{2,1,0:T(8,128)(2,1)S(1)}, u32[]{:S(2)}, u32[]{:S(2)}) async-start(bf16[8,208,256]{2,1,0:T(8,128)(2,1)} %pad_maximum_fusion.3), calls=%async_computation.10 | async-start | bytes 1703936 | tf_op jit(solution)/shard_map/all_to_all | solution.py:406
  373.7 141.9 %all-gather.10.cloned.1.call-start = ((), (), s32[]{:S(2)}) async-start(), calls=%async_computation.17 | async-start | bytes 5898240 | tf_op jit(solution)/shard_map/all_gather | solution.py:689
  378.2 9.3 %copy-start.42 = (pred[40,256]{1,0:T(8,128)(4,1)S(1)}, pred[40,256]{1,0:T(8,128)(4,1)}, u32[]{:S(2)}) copy-start(pred[40,256]{1,0:T(8,128)(4,1)} %copy-done.41) | copy-start | bytes 30724
  378.2 9.3 %copy-start.46 = (f32[40,256]{1,0:T(8,128)S(1)}, f32[40,256]{1,0:T(8,128)}, u32[]{:S(2)}) copy-start(f32[40,256]{1,0:T(8,128)} %copy-done.45) | copy-start | bytes 122884
  378.2 9.3 %copy-start.90 = (f32[256]{0:T(256)S(1)}, f32[256]{0:T(256)}, u32[]{:S(2)}) copy-start(f32[256]{0:T(256)} %copy-done.89) | copy-start | bytes 3076
  378.2 9.3 %copy-start.92 = (f32[256]{0:T(256)S(1)}, f32[256]{0:T(256)}, u32[]{:S(2)}) copy-start(f32[256]{0:T(256)} %copy-done.91) | copy-start | bytes 3076
  378.2 9.4 %copy-start.116 = (f32[256]{0:T(256)S(1)}, f32[256]{0:T(256)}, u32[]{:S(2)}) copy-start(f32[256]{0:T(256)} %copy-done.115) | copy-start | bytes 3076
  378.2 9.4 %copy-start.67 = (bf16[1,192,40]{1,2,0:T(8,128)(2,1)S(1)}, bf16[1,192,40]{1,2,0:T(8,128)(2,1)}, u32[]{:S(2)}) copy-start(bf16[1,192,40]{1,2,0:T(8,128)(2,1)} %param.15) | copy-start | bytes 46084
  392.3 27.0 %all-to-all-start.11 = ((bf16[8,192,274]{1,2,0:T(8,128)(2,1)}), bf16[8,192,274]{1,2,0:T(8,128)(2,1)S(1)}, u32[]{:S(2)}, u32[]{:S(2)}) async-start(bf16[8,192,274]{1,2,0:T(8,128)(2,1)} %pad_maximum_fusion.1), calls=%async_computation.11 | async-start | bytes 2293760 | tf_op jit(solution)/shard_map/all_to_all | solution.py:406
  399.1 22.7 %copy-start.2 = (bf16[8,128,256]{2,1,0:T(8,128)(2,1)S(1)}, bf16[8,128,256]{2,1,0:T(8,128)(2,1)}, u32[]{:S(2)}) copy-start(bf16[8,128,256]{2,1,0:T(8,128)(2,1)} %copy-done.1) | copy-start | bytes 1572868
  399.1 22.7 %copy-start.16 = (f32[3,1,256]{2,1,0:T(1,128)S(1)}, f32[3,1,256]{2,1,0:T(1,128)}, u32[]{:S(2)}) copy-start(f32[3,1,256]{2,1,0:T(1,128)} %copy-done.15) | copy-start | bytes 9220
  419.3 6.5 %copy-start.30 = (bf16[8,192,274]{1,2,0:T(8,128)(2,1)}, bf16[8,192,274]{1,2,0:T(8,128)(2,1)S(1)}, u32[]{:S(2)}) copy-start(bf16[8,192,274]{1,2,0:T(8,128)(2,1)S(1)} %all-to-all-done.11) | copy-start | bytes 2525188
  425.8 15.7 %all-to-all-start.12 = ((bf16[8,128,256]{2,1,0:T(8,128)(2,1)}), bf16[8,128,256]{2,1,0:T(8,128)(2,1)S(1)}, u32[]{:S(2)}, u32[]{:S(2)}) async-start(bf16[8,128,256]{2,1,0:T(8,128)(2,1)} %get-tuple-element.79), calls=%async_computation.12 | async-start | bytes 1048576 | tf_op jit(solution)/shard_map/all_to_all | solution.py:406
  441.5 7.4 %copy-start.58 = (f32[32,256]{1,0:T(8,128)S(1)}, f32[32,256]{1,0:T(8,128)}, u32[]{:S(2)}) copy-start(f32[32,256]{1,0:T(8,128)} %copy-done.56) | copy-start | bytes 98308
  441.5 7.5 %copy-start.73 = (f32[32,256]{1,0:T(8,128)S(1)}, f32[32,256]{1,0:T(8,128)}, u32[]{:S(2)}) copy-start(f32[32,256]{1,0:T(8,128)} %copy-done.72) | copy-start | bytes 98308
  442.3 17.7 %all-to-all-start.4 = ((bf16[8,192,256]{2,1,0:T(8,128)(2,1)}), bf16[8,192,256]{2,1,0:T(8,128)(2,1)S(1)}, u32[]{:S(2)}, u32[]{:S(2)}) async-start(bf16[8,192,256]{2,1,0:T(8,128)(2,1)} %bitcast.37), calls=%async_computation.4 | async-start | bytes 1572864 | tf_op jit(solution)/shard_map/all_to_all | solution.py:406
  461.2 23.0 %all-to-all-start.13 = ((bf16[8,336,256]{2,1,0:T(8,128)(2,1)}), bf16[8,336,256]{2,1,0:T(8,128)(2,1)S(1)}, u32[]{:S(2)}, u32[]{:S(2)}) async-start(bf16[8,336,256]{2,1,0:T(8,128)(2,1)} %broadcast_in_dim.211), calls=%async_computation.13 | async-start | bytes 2752512 | tf_op jit(solution)/shard_map/all_to_all | solution.py:406
  465.5 18.9 %copy-start.105 = (f32[256]{0:T(256)S(1)}, f32[256]{0:T(256)}, u32[]{:S(2)}) copy-start(f32[256]{0:T(256)} %copy-done.104) | copy-start | bytes 3076
  465.5 18.9 %copy-start.27 = (bf16[1,192,2560]{2,1,0:T(8,128)(2,1)S(1)}, bf16[1,192,2560]{2,1,0:T(8,128)(2,1)}, u32[]{:S(2)}) copy-start(bf16[1,192,2560]{2,1,0:T(8,128)(2,1)} %param.13) | copy-start | bytes 2949124
  465.5 18.9 %copy-start.60 = (bf16[192,128]{1,0:T(8,128)(2,1)S(1)}, bf16[192,128]{1,0:T(8,128)(2,1)}, u32[]{:S(2)}) copy-start(bf16[192,128]{1,0:T(8,128)(2,1)} %copy-done.59) | copy-start | bytes 147460
  465.5 18.9 %copy-start.97 = (f32[256]{0:T(256)S(1)}, f32[256]{0:T(256)}, u32[]{:S(2)}) copy-start(f32[256]{0:T(256)} %copy-done.96) | copy-start | bytes 3076
  466.3 18.1 %copy-start.62 = (bf16[192,128]{1,0:T(8,128)(2,1)S(1)}, bf16[192,128]{1,0:T(8,128)(2,1)}, u32[]{:S(2)}) copy-start(bf16[192,128]{1,0:T(8,128)(2,1)} %copy-done.61) | copy-start | bytes 147460
  493.4 20.5 %all-to-all-start.14 = ((bf16[8,192,322]{2,1,0:T(8,128)(2,1)}), bf16[8,192,322]{2,1,0:T(8,128)(2,1)S(1)}, u32[]{:S(2)}, u32[]{:S(2)}) async-start(bf16[8,192,322]{2,1,0:T(8,128)(2,1)} %pad_maximum_fusion), calls=%async_computation.14 | async-start | bytes 2359296 | tf_op jit(solution)/shard_map/all_to_all | solution.py:406
  (75 other events, 136.5 us)
Sparse Core Ops, SparseCore 0:
  45.5 35.0 all-gather.5
  240.7 66.3 all-gather.7
  376.8 92.6 all-gather.9
